TPU v7x, 512 devices: a whole 4x4x16 slice. The times are simulated.
512 devices in a mesh: dp: 64 (over z, x), mp: 8 (over y, core).
Axes of the slice: x: 4, y: 4, z: 16, core: 2. Of those that a mesh axis runs over, the one named last changes fastest.
Arguments:
- query_rows: bfloat16 [49152, 4096], P('dp', 'mp')
- key_rows: bfloat16 [49152, 1024], P('dp', 'mp')
- value_rows: bfloat16 [49152, 1024], P('dp', 'mp'), may hold values from -6 to 6
- grad_rows: bfloat16 [49152, 4096], P('dp', 'mp'), may hold values from -6 to 6
- doc_ids: int32 [49152], P('dp'), may hold values from 0 to 383, as said below
- leaving_group: int32 [64], P('dp'), may hold values from 0 to 1
Outputs:
- attended: bfloat16 [49152, 4096], P('dp', 'mp')
- grad_query: bfloat16 [49152, 4096], P('dp', 'mp')
- grad_key: bfloat16 [49152, 1024], P('dp', 'mp')
- grad_value: bfloat16 [49152, 1024], P('dp', 'mp')
Inputs may be any that keep to these rules, and one draw needn't show every extreme that they name: `doc_ids`: in each aligned run of 384 rows the numbers start at 0 and never fall; equal numbers in a run are one document.
All inputs are finite; a program needn't handle non-finite values.
Results may differ from a plain program's by a relative error of at most 0.018.
Values may be sent and summed in bfloat16 or wider, within the bound.
No kernel may reach another device: no remote copies, remote signals or barrier semaphores. Data moves between devices by JAX's collectives and lax.ppermute only.
A program may use at most 64 MiB of HBM per device.

v0:
```python
import jax
import jax.numpy as jnp
from jax import lax
from jax.sharding import PartitionSpec as P

HEAD_DIM = 128
SLOT = 384


def as_sent(x):

    def short(part):
        return part.astype(jnp.bfloat16) if part.dtype == jnp.float32 else part

    return jax.tree.map(short, x)


def swapped(x, axis, bit):
    return lax.ppermute(x, axis, [(i, i ^ 1 << bit) for i in range(lax.axis_size(axis))])


def attend(queries, key_block, value_block, grad_block, doc_marks):
    length = queries.shape[0]
    kv_local = key_block.shape[1] // HEAD_DIM
    scaling = HEAD_DIM ** (-0.5)
    query_mat = queries.reshape(length, kv_local, -1, HEAD_DIM)
    key_mat = key_block.reshape(length, kv_local, HEAD_DIM)
    value_mat = value_block.reshape(length, kv_local, HEAD_DIM)
    grad_mat = grad_block.reshape(length, kv_local, -1, HEAD_DIM)
    places = jnp.arange(length)
    allowed = (doc_marks[:, None] == doc_marks[None, :]) & (places[None, :] <= places[:, None])
    scores = (
        jnp.einsum("igqd,jgd->gqij", query_mat, key_mat, preferred_element_type=jnp.float32)
        * scaling
    )
    scores = jnp.where(allowed[None, None], scores, jnp.float32(-1e30))
    row_max = jnp.max(scores, axis=-1, keepdims=True)
    weights = jnp.exp(scores - row_max)
    probs = weights / jnp.sum(weights, axis=-1, keepdims=True)
    probs16 = probs.astype(jnp.bfloat16)
    attended = jnp.einsum(
        "gqij,jgd->igqd", probs16, value_mat, preferred_element_type=jnp.float32
    ).astype(jnp.bfloat16)
    dprobs = jnp.einsum("igqd,jgd->gqij", grad_mat, value_mat, preferred_element_type=jnp.float32)
    inner_sum = jnp.sum(probs * dprobs, axis=-1, keepdims=True)
    dscores = (probs * (dprobs - inner_sum)).astype(jnp.bfloat16)
    grad_query = (
        jnp.einsum("gqij,jgd->igqd", dscores, key_mat, preferred_element_type=jnp.float32) * scaling
    ).astype(jnp.bfloat16)
    grad_key = (
        jnp.einsum("gqij,igqd->jgd", dscores, query_mat, preferred_element_type=jnp.float32)
        * scaling
    ).astype(jnp.bfloat16)
    grad_value = jnp.einsum(
        "gqij,igqd->jgd", probs16, grad_mat, preferred_element_type=jnp.float32
    ).astype(jnp.bfloat16)
    return (
        attended.reshape(length, -1),
        grad_query.reshape(length, -1),
        grad_key.reshape(length, -1),
        grad_value.reshape(length, -1),
    )


def body(query_rows, key_rows, value_rows, grad_rows, doc_ids, leaving_group):
    row_count = query_rows.shape[0]
    group_count = row_count // SLOT
    chosen_slot = leaving_group[0]

    def grouped(tensor):
        return tensor.reshape((group_count, SLOT) + tensor.shape[1:])

    doc_marks = doc_ids.reshape(group_count, SLOT)
    changes = (doc_marks[:, 1:] != doc_marks[:, :-1]).astype(jnp.int32)
    boundary_flags = jnp.concatenate([jnp.zeros((group_count, 1), jnp.int32), changes], axis=1)
    holding = (
        grouped(query_rows),
        grouped(key_rows),
        grouped(value_rows),
        grouped(grad_rows),
        boundary_flags.astype(jnp.bfloat16),
    )

    def selected(tensor):
        return lax.dynamic_index_in_dim(tensor, chosen_slot, 0, keepdims=False)

    def inserted(tensor, fresh):
        return lax.dynamic_update_index_in_dim(tensor, fresh, chosen_slot, 0)

    far_bit = lax.axis_size("dp").bit_length() - 2
    local_marks = jnp.cumsum(holding[4].astype(jnp.int32), axis=1)

    def one_group(which):
        pieces = tuple(
            (lax.dynamic_index_in_dim(tensor, which, 0, keepdims=False) for tensor in holding[:4])
        )
        marks_here = lax.dynamic_index_in_dim(local_marks, which, 0, keepdims=False)
        return attend(pieces[0], pieces[1], pieces[2], pieces[3], marks_here)

    results = lax.map(one_group, jnp.arange(group_count))
    outgoing = tuple((selected(tensor) for tensor in results))
    returned = jax.tree.map(
        lambda part, own: part.astype(own.dtype),
        swapped(as_sent(outgoing), "dp", far_bit),
        outgoing,
    )
    final = tuple(
        (inserted(tensor, fresh).reshape(row_count, -1) for tensor, fresh in zip(results, returned))
    )
    return (final[0], final[1], final[2], final[3])


def solution(mesh):
    return jax.shard_map(
        body,
        mesh=mesh,
        in_specs=(P("dp", "mp"), P("dp", "mp"), P("dp", "mp"), P("dp", "mp"), P("dp"), P("dp")),
        out_specs=(P("dp", "mp"), P("dp", "mp"), P("dp", "mp"), P("dp", "mp")),
        check_vma=False,
    )
```

profile of v0, /device:TPU:1, one launch (start us, length us, event | category | flops | bytes accessed | tf_op | source)
XLA Modules:
  0.0 143.3 jit_solution(10430977331410178960)
XLA Ops:
  3.3 31.1 %while.16 = (s32[]{:T(128)}, bf16[2,384,512]{1,2,0:T(8,128)(2,1)}, bf16[2,384,512]{1,2,0:T(8,128)(2,1)}, bf16[2,384,128]{1,2,0:T(8,128)(2,1)S(1)}, bf16[2,384,12...) while((s32[]{:T(128)}, bf16[2,384,512]{1,2,0:T(8,128)(2,1)}, ...), condition=%wide.region_6.7_spmd, body=%wide.region_2.6_spmd.sunk | while | flops 924839424 | bytes 50073012 | solution.py:100
  6.2 1.0 constant_dynamic-slice_fusion.5
  7.5 1.5 %fusion.85 = (f32[4,384]{1,0:T(4,128)S(1)}, f32[384,384,4]{1,0,2:T(8,128)S(1)}) fusion(pred[384,384]{0,1:T(8,128)(4,1)S(1)} %fusion.84, bf16[384,4,128]{0,2,1:T(8,128)(2,1)S(1)} %bitcast.219, bf16[2,384,128]{2,1,0:T(8,128)(2,1)} %get-tuple-element.233, s32[]{:T(128)S(6)} %select_n.59), kind=kOutput, calls=%fused_computation.9.clone.1 | convolution fusion | flops 152762880 | bytes 3004420 | tf_op jit(solution)/shard_map/while/body/eval_jaxpr/igqd,jgd->gqij/dot_general | solution.py:33
  9.5 0.9 copy.69
  10.4 2.5 %fusion.91 = bf16[2,384,128]{1,2,0:T(8,128)(2,1)} fusion(bf16[2,384,128]{1,2,0:T(8,128)(2,1)} %get-tuple-element.215, s32[]{:T(128)} %get-tuple-element.211, bf16[384,4,128]{0,2,1:T(8,128)(2,1)} %bitcast.222, f32[4,384]{1,0:T(4,128)S(1)} %fusion.86, f32[4,384]{1,0:T(4,128)S(1)} %get-tuple-element.192, f32[384,384,4]{1,0,2:T(8,128)S(1)} %get-tuple-element.191, ...), kind=kOutput, calls=%fused_computation.23.clone.1 | convolution fusion | flops 153993216 | bytes 3011072 | tf_op jit(solution)/shard_map/while/body/eval_jaxpr/gqij,igqd->jgd/dot_general | solution.py:54
  14.0 0.9 fusion.87
  16.6 0.9 copy-done.4
  17.4 0.9 copy-done.7
  21.7 1.0 constant_dynamic-slice_fusion.5
  23.0 1.5 %fusion.85 = (f32[4,384]{1,0:T(4,128)S(1)}, f32[384,384,4]{1,0,2:T(8,128)S(1)}) fusion(pred[384,384]{0,1:T(8,128)(4,1)S(1)} %fusion.84, bf16[384,4,128]{0,2,1:T(8,128)(2,1)S(1)} %bitcast.219, bf16[2,384,128]{2,1,0:T(8,128)(2,1)} %get-tuple-element.233, s32[]{:T(128)S(6)} %select_n.59), kind=kOutput, calls=%fused_computation.9.clone.1 | convolution fusion | flops 152762880 | bytes 3004420 | tf_op jit(solution)/shard_map/while/body/eval_jaxpr/igqd,jgd->gqij/dot_general | solution.py:33
  25.1 0.9 copy.69
  26.0 2.5 %fusion.91 = bf16[2,384,128]{1,2,0:T(8,128)(2,1)} fusion(bf16[2,384,128]{1,2,0:T(8,128)(2,1)} %get-tuple-element.215, s32[]{:T(128)} %get-tuple-element.211, bf16[384,4,128]{0,2,1:T(8,128)(2,1)} %bitcast.222, f32[4,384]{1,0:T(4,128)S(1)} %fusion.86, f32[4,384]{1,0:T(4,128)S(1)} %get-tuple-element.192, f32[384,384,4]{1,0,2:T(8,128)S(1)} %get-tuple-element.191, ...), kind=kOutput, calls=%fused_computation.23.clone.1 | convolution fusion | flops 153993216 | bytes 3011072 | tf_op jit(solution)/shard_map/while/body/eval_jaxpr/gqij,igqd->jgd/dot_general | solution.py:54
  29.5 0.9 fusion.87
  33.0 0.9 copy-done.7
  34.4 1.1 dynamic-slice_bitcast_fusion
  35.5 16.3 %collective-permute-start.1 = (bf16[384,512]{0,1:T(8,128)(2,1)S(1)}, bf16[384,512]{0,1:T(8,128)(2,1)S(1)}, u32[]{:S(2)}, u32[]{:S(2)}) collective-permute-start(bf16[384,512]{0,1:T(8,128)(2,1)S(1)} %dynamic-slice_bitcast_fusion), channel_id=1, source_target_pairs={{0,256},{8,264},{16,272},{24,280},{32,288},{40,296},{48,304},{56,3... | collective-permute-start | bytes 1179656 | tf_op jit(solution)/shard_map/ppermute | solution.py:19
  51.8 2.1 %collective-permute-start.2 = (bf16[384,128]{0,1:T(8,128)(2,1)S(1)}, bf16[384,128]{0,1:T(8,128)(2,1)S(1)}, u32[]{:S(2)}, u32[]{:S(2)}) collective-permute-start(bf16[384,128]{0,1:T(8,128)(2,1)S(1)} %dynamic-slice_bitcast_fusion.3), channel_id=1, source_target_pairs={{0,256},{8,264},{16,272},{24,280},{32,288},{40,296},{48,304},{56,3... | collective-permute-start | bytes 294920 | tf_op jit(solution)/shard_map/ppermute | solution.py:19
  53.9 0.9 dynamic-slice_bitcast_fusion.2
  54.8 12.1 %collective-permute-start.3 = (bf16[384,128]{0,1:T(8,128)(2,1)S(1)}, bf16[384,128]{0,1:T(8,128)(2,1)S(1)}, u32[]{:S(2)}, u32[]{:S(2)}) collective-permute-start(bf16[384,128]{0,1:T(8,128)(2,1)S(1)} %dynamic-slice_bitcast_fusion.2), channel_id=1, source_target_pairs={{0,256},{8,264},{16,272},{24,280},{32,288},{40,296},{48,304},{56,3... | collective-permute-start | bytes 294920 | tf_op jit(solution)/shard_map/ppermute | solution.py:19
  66.9 1.8 %dynamic-slice_bitcast_fusion.1 = bf16[384,512]{0,1:T(8,128)(2,1)} fusion(bf16[2,384,512]{1,2,0:T(8,128)(2,1)} %get-tuple-element.64, s32[]{:T(128)S(6)} %select_n.26), kind=kLoop, calls=%fused_computation.52 | loop fusion | bytes 786436 | tf_op jit(solution)/shard_map/jit(dynamic_index_in_dim)/squeeze | solution.py:85
  68.7 1.9 %collective-permute-start = (bf16[384,512]{0,1:T(8,128)(2,1)}, bf16[384,512]{0,1:T(8,128)(2,1)S(1)}, u32[]{:S(2)}, u32[]{:S(2)}) collective-permute-start(bf16[384,512]{0,1:T(8,128)(2,1)} %dynamic-slice_bitcast_fusion.1), channel_id=1, source_target_pairs={{0,256},{8,264},{16,272},{24,280},{32,288},{40,296},{48,304},{56,3... | collective-permute-start | bytes 1179656 | tf_op jit(solution)/shard_map/ppermute | solution.py:19
  72.4 1.2 copy.47
  73.6 68.5 %collective-permute-done = bf16[384,512]{0,1:T(8,128)(2,1)S(1)} collective-permute-done((bf16[384,512]{0,1:T(8,128)(2,1)}, bf16[384,512]{0,1:T(8,128)(2,1)S(1)}, u32[]{:S(2)}, u32[]{:S(2)}) %collective-permute-start) | collective-permute-done | bytes 393248 | tf_op jit(solution)/shard_map/ppermute | solution.py:19
  142.1 1.2 copy.46
  (81 shorter events, 14.1 us)
Async XLA Ops:
  7.4 2.0 %copy-start.2 = (bf16[2,384,512]{2,1,0:T(8,128)(2,1)S(1)}, bf16[2,384,512]{2,1,0:T(8,128)(2,1)}, u32[]{:S(2)}) copy-start(bf16[2,384,512]{2,1,0:T(8,128)(2,1)} %get-tuple-element.235) | copy-start | bytes 2359300 | tf_op jit(solution)/shard_map/while
  10.4 2.5 %copy-start.10 = (bf16[2,384,128]{2,1,0:T(8,128)(2,1)S(1)}, bf16[2,384,128]{2,1,0:T(8,128)(2,1)}, u32[]{:S(2)}) copy-start(bf16[2,384,128]{2,1,0:T(8,128)(2,1)} %get-tuple-element.231) | copy-start | bytes 589828 | tf_op jit(solution)/shard_map/while
  13.0 1.0 copy-start
  14.9 0.9 copy-start.1
  14.9 1.3 copy-start.3
  14.9 1.5 %copy-start.6 = (bf16[2,384,512]{1,2,0:T(8,128)(2,1)S(1)}, bf16[2,384,512]{1,2,0:T(8,128)(2,1)}, u32[]{:S(2)}) copy-start(bf16[2,384,512]{1,2,0:T(8,128)(2,1)} %get-tuple-element.213) | copy-start | bytes 2359300 | tf_op jit(solution)/shard_map/while
  16.5 0.9 copy-start.4
  17.4 0.9 copy-start.7
  23.0 2.0 %copy-start.2 = (bf16[2,384,512]{2,1,0:T(8,128)(2,1)S(1)}, bf16[2,384,512]{2,1,0:T(8,128)(2,1)}, u32[]{:S(2)}) copy-start(bf16[2,384,512]{2,1,0:T(8,128)(2,1)} %get-tuple-element.235) | copy-start | bytes 2359300 | tf_op jit(solution)/shard_map/while
  26.0 2.5 %copy-start.10 = (bf16[2,384,128]{2,1,0:T(8,128)(2,1)S(1)}, bf16[2,384,128]{2,1,0:T(8,128)(2,1)}, u32[]{:S(2)}) copy-start(bf16[2,384,128]{2,1,0:T(8,128)(2,1)} %get-tuple-element.231) | copy-start | bytes 589828 | tf_op jit(solution)/shard_map/while
  28.5 1.0 copy-start
  30.4 0.9 copy-start.1
  30.4 1.3 copy-start.3
  30.4 1.5 %copy-start.6 = (bf16[2,384,512]{1,2,0:T(8,128)(2,1)S(1)}, bf16[2,384,512]{1,2,0:T(8,128)(2,1)}, u32[]{:S(2)}) copy-start(bf16[2,384,512]{1,2,0:T(8,128)(2,1)} %get-tuple-element.213) | copy-start | bytes 2359300 | tf_op jit(solution)/shard_map/while
  32.1 0.9 copy-start.4
  33.0 0.9 copy-start.7
  34.4 37.1 %copy-start.9 = (bf16[2,384,128]{1,2,0:T(8,128)(2,1)S(1)}, bf16[2,384,128]{1,2,0:T(8,128)(2,1)}, u32[]{:S(2)}) copy-start(bf16[2,384,128]{1,2,0:T(8,128)(2,1)} %get-tuple-element.67) | copy-start | bytes 589828
  34.4 37.9 %copy-start.8 = (bf16[2,384,512]{1,2,0:T(8,128)(2,1)S(1)}, bf16[2,384,512]{1,2,0:T(8,128)(2,1)}, u32[]{:S(2)}) copy-start(bf16[2,384,512]{1,2,0:T(8,128)(2,1)} %get-tuple-element.65) | copy-start | bytes 2359300
  35.5 36.8 %collective-permute-start.1 = (bf16[384,512]{0,1:T(8,128)(2,1)S(1)}, bf16[384,512]{0,1:T(8,128)(2,1)S(1)}, u32[]{:S(2)}, u32[]{:S(2)}) collective-permute-start(bf16[384,512]{0,1:T(8,128)(2,1)S(1)} %dynamic-slice_bitcast_fusion), channel_id=1, source_target_pairs={{0,256},{8,264},{16,272},{24,280},{32,288},{40,296},{48,304},{56,3... | collective-permute-start | bytes 1179656 | tf_op jit(solution)/shard_map/ppermute | solution.py:19
  51.8 90.3 %copy-start.5 = (bf16[2,384,512]{1,2,0:T(8,128)(2,1)S(1)}, bf16[2,384,512]{1,2,0:T(8,128)(2,1)}, u32[]{:S(2)}) copy-start(bf16[2,384,512]{1,2,0:T(8,128)(2,1)} %get-tuple-element.64) | copy-start | bytes 2359300
  51.8 18.8 %collective-permute-start.2 = (bf16[384,128]{0,1:T(8,128)(2,1)S(1)}, bf16[384,128]{0,1:T(8,128)(2,1)S(1)}, u32[]{:S(2)}, u32[]{:S(2)}) collective-permute-start(bf16[384,128]{0,1:T(8,128)(2,1)S(1)} %dynamic-slice_bitcast_fusion.3), channel_id=1, source_target_pairs={{0,256},{8,264},{16,272},{24,280},{32,288},{40,296},{48,304},{56,3... | collective-permute-start | bytes 294920 | tf_op jit(solution)/shard_map/ppermute | solution.py:19
  54.8 16.6 %collective-permute-start.3 = (bf16[384,128]{0,1:T(8,128)(2,1)S(1)}, bf16[384,128]{0,1:T(8,128)(2,1)S(1)}, u32[]{:S(2)}, u32[]{:S(2)}) collective-permute-start(bf16[384,128]{0,1:T(8,128)(2,1)S(1)} %dynamic-slice_bitcast_fusion.2), channel_id=1, source_target_pairs={{0,256},{8,264},{16,272},{24,280},{32,288},{40,296},{48,304},{56,3... | collective-permute-start | bytes 294920 | tf_op jit(solution)/shard_map/ppermute | solution.py:19
  68.7 73.4 %collective-permute-start = (bf16[384,512]{0,1:T(8,128)(2,1)}, bf16[384,512]{0,1:T(8,128)(2,1)S(1)}, u32[]{:S(2)}, u32[]{:S(2)}) collective-permute-start(bf16[384,512]{0,1:T(8,128)(2,1)} %dynamic-slice_bitcast_fusion.1), channel_id=1, source_target_pairs={{0,256},{8,264},{16,272},{24,280},{32,288},{40,296},{48,304},{56,3... | collective-permute-start | bytes 1179656 | tf_op jit(solution)/shard_map/ppermute | solution.py:19
where the time goes:
time: 144 us; the launch traced here: 143 us
  waiting for transfers between devices  68.5 us (48%)
  starting transfers between devices  32.3 us (22%)
  local copies, waits for them, and re-layouts  19.4 us (13%)
  matrix products  13.4 us (9%)
  loops' own time  4.42 us (3%)
  other arithmetic  3.81 us (3%)
    ppermute x4, waiting for transfers between devices, swapped(): lax.ppermute(x, axis, [(i, i ^ 1 << bit) for i in range(lax.axis_size(axi...  68.5 us
    ppermute x4, starting transfers between devices, swapped(): lax.ppermute(x, axis, [(i, i ^ 1 << bit) for i in range(lax.axis_size(axi...  32.3 us
    dot_general x2, matrix products, attend(): jnp.einsum('gqij,igqd->jgd', probs16, grad_mat, preferred_element_type=jn...  5.05 us
    another operation x1, loops' own time, body(): results = lax.map(one_group, jnp.arange(group_count))  4.42 us
    while x32, local copies, waits for them, and re-layouts  4.37 us
    dynamic_slice x8, local copies, waits for them, and re-layouts, one_group(): lax.dynamic_index_in_dim(tensor, which, 0, keepdims=False)  4.37 us
    dynamic_update_slice x8, local copies, waits for them, and re-layouts, inserted(): return lax.dynamic_update_index_in_dim(tensor, fresh, chosen_slot, 0)  4.17 us
    squeeze x4, local copies, waits for them, and re-layouts, selected(): return lax.dynamic_index_in_dim(tensor, chosen_slot, 0, keepdims=False)  3.83 us
  transfers between devices with their start and end apart: 4, of which 1 were waited for; matrix products, arithmetic and copies ran while one was open for 4% of the time, Pallas kernels for 0%

commit v1 on v0

v1 whole, which is shorter than its diff:
```python
import functools

import jax
import jax.numpy as jnp
from jax import lax
from jax.experimental import pallas as pl
from jax.experimental.pallas import tpu as pltpu
from jax.sharding import PartitionSpec as P

HEAD_DIM = 128
SLOT = 384
ROWS = 128
STEPS = SLOT // ROWS
LOG2E = 1.4426950408889634
SCALING = HEAD_DIM ** (-0.5)
MASKED = -1e30 * LOG2E


def swapped(x, axis, bit):
    return lax.ppermute(x, axis, [(i, i ^ 1 << bit) for i in range(lax.axis_size(axis))])


def pack_kernel(slot_ref, q_ref, g_ref, k_ref, v_ref, out_ref, sems):
    heads = q_ref.shape[1] // HEAD_DIM
    base = pl.multiple_of(slot_ref[0] * SLOT, SLOT)
    rows = pl.ds(base, SLOT)
    parts = [q_ref.at[rows, pl.ds(h * HEAD_DIM, HEAD_DIM)] for h in range(heads)]
    parts += [g_ref.at[rows, pl.ds(h * HEAD_DIM, HEAD_DIM)] for h in range(heads)]
    parts += [k_ref.at[rows], v_ref.at[rows]]
    copies = [
        pltpu.make_async_copy(part, out_ref.at[i], sems.at[i]) for i, part in enumerate(parts)
    ]
    for copy in copies:
        copy.start()
    for copy in copies:
        copy.wait()


def pack(slot, query, grad, key, value):
    heads = query.shape[1] // HEAD_DIM
    count = 2 * heads + 2
    return pl.pallas_call(
        pack_kernel,
        out_shape=jax.ShapeDtypeStruct((count, SLOT, HEAD_DIM), query.dtype),
        in_specs=[pl.BlockSpec(memory_space=pltpu.SMEM)]
        + [pl.BlockSpec(memory_space=pltpu.HBM)] * 4,
        out_specs=pl.BlockSpec(memory_space=pl.ANY),
        scratch_shapes=[pltpu.SemaphoreType.DMA((count,))],
        name="pack_leaving",
    )(slot, query, grad, key, value)


def attend_block(step, ids, q, g, k_ref, v_ref, kt, vt, dk_acc, dv_acc, write):
    span = SLOT
    heads = len(q)
    q_all = jnp.concatenate(q, axis=0)
    g_all = jnp.concatenate(g, axis=0)
    keys, values = k_ref[:span, :], v_ref[:span, :]
    over_rows = (((1,), (1,)), ((), ()))
    scores = lax.dot_general(keys, q_all, over_rows, preferred_element_type=jnp.float32)
    dprobs = lax.dot_general(values, g_all, over_rows, preferred_element_type=jnp.float32)
    ids_t = ids.T
    key_ids = jnp.concatenate([ids_t[:, j : j + 1] for j in range(span // ROWS)], axis=0)
    places_j = lax.broadcasted_iota(jnp.int32, (span, ROWS), 0)
    places_i = lax.broadcasted_iota(jnp.int32, (span, ROWS), 1) + step * ROWS
    allowed = (key_ids == ids[step : step + 1, :]) & (places_j <= places_i)
    allowed = jnp.concatenate([allowed] * heads, axis=1)
    scores = jnp.where(allowed, scores * (SCALING * LOG2E), MASKED)
    weights = jnp.exp2(scores - jnp.max(scores, axis=0, keepdims=True))
    probs = weights * (1.0 / jnp.sum(weights, axis=0, keepdims=True))
    inner_sum = jnp.sum(probs * dprobs, axis=0, keepdims=True)
    probs16 = probs.astype(jnp.bfloat16)
    dscores = (probs * (dprobs - inner_sum)).astype(jnp.bfloat16)
    dv = jnp.dot(probs16, g_all, preferred_element_type=jnp.float32)
    dk = jnp.dot(dscores, q_all, preferred_element_type=jnp.float32)
    if step == 0:
        dv_acc[...] = dv
        dk_acc[...] = dk
    else:
        dv_acc[...] += dv
        dk_acc[...] += dk
    out_t = jnp.dot(vt[:, :span], probs16, preferred_element_type=jnp.float32)
    dq_t = jnp.dot(kt[:, :span], dscores, preferred_element_type=jnp.float32) * SCALING
    for h in range(heads):
        cols = slice(h * ROWS, (h + 1) * ROWS)
        write(h, out_t[:, cols].T.astype(jnp.bfloat16), dq_t[:, cols].T.astype(jnp.bfloat16))


def attend_kernel(received, slot_ref, docs_ref, q_ref, g_ref, k_ref, v_ref, *rest):
    if received:
        rest = rest[4:]
    o_ref, dq_ref, dk_ref, dv_ref, kt, vt, dk_acc, dv_acc = rest
    heads = o_ref.shape[1] // HEAD_DIM

    def lanes(h):
        return slice(h * HEAD_DIM, (h + 1) * HEAD_DIM)

    if received:
        marks = docs_ref[...].astype(jnp.float32)
        ids = marks[:8] * 16.0 + marks[8:]
        k_ref, v_ref = k_ref.at[0], v_ref.at[0]
    else:
        ids = docs_ref[0]

    def write(h, out, dq):
        o_ref[:, lanes(h)] = out
        dq_ref[:, lanes(h)] = dq

    index = pl.program_id(0)

    @pl.when(index == 0)
    def _():
        kt[...] = k_ref[...].T
        vt[...] = v_ref[...].T

    for step in range(STEPS):

        @pl.when(index == step)
        def _():
            if received:
                q = [q_ref[h] for h in range(heads)]
                g = [g_ref[h] for h in range(heads)]
            else:
                q = [q_ref[:, lanes(h)] for h in range(heads)]
                g = [g_ref[:, lanes(h)] for h in range(heads)]
            attend_block(step, ids, q, g, k_ref, v_ref, kt, vt, dk_acc, dv_acc, write)

    @pl.when(index == STEPS - 1)
    def _():
        dk_ref[...] = (dk_acc[...] * SCALING).astype(jnp.bfloat16)
        dv_ref[...] = dv_acc[...].astype(jnp.bfloat16)


def attend(slot, docs, inputs, in_specs, row_count, width, kv_width, held=None):
    received = held is not None
    any_spec = pl.BlockSpec(memory_space=pl.ANY)
    wide = pl.BlockSpec((ROWS, width), lambda i, s: (s[0] * STEPS + i, 0))
    narrow = pl.BlockSpec((SLOT, kv_width), lambda i, s: (s[0], 0))
    shapes = [(row_count, width)] * 2 + [(row_count, kv_width)] * 2
    work = 12 * (width // HEAD_DIM) * SLOT * SLOT * HEAD_DIM
    return pl.pallas_call(
        functools.partial(attend_kernel, received),
        out_shape=tuple(jax.ShapeDtypeStruct(shape, jnp.bfloat16) for shape in shapes),
        grid_spec=pltpu.PrefetchScalarGridSpec(
            num_scalar_prefetch=1,
            grid=(STEPS,),
            in_specs=in_specs + ([any_spec] * 4 if received else []),
            out_specs=(wide, wide, narrow, narrow),
            scratch_shapes=[
                pltpu.VMEM((HEAD_DIM, SLOT), jnp.bfloat16),
                pltpu.VMEM((HEAD_DIM, SLOT), jnp.bfloat16),
                pltpu.VMEM((SLOT, HEAD_DIM), jnp.float32),
                pltpu.VMEM((SLOT, HEAD_DIM), jnp.float32),
            ],
        ),
        input_output_aliases={6 + i: i for i in range(4)} if received else {},
        compiler_params=pltpu.CompilerParams(vmem_limit_bytes=24 * 1024 * 1024),
        cost_estimate=pl.CostEstimate(
            flops=work, bytes_accessed=4 * 1024 * 1024, transcendentals=SLOT * SLOT * 4
        ),
        name="attend_received" if received else "attend_staying",
    )(slot, docs, *inputs, *(held if received else ()))


def body(query_rows, key_rows, value_rows, grad_rows, doc_ids, leaving_group):
    row_count, width = query_rows.shape
    kv_width = key_rows.shape[1]
    heads = width // HEAD_DIM
    group_count = row_count // SLOT
    far_bit = lax.axis_size("dp").bit_length() - 2
    staying = group_count - 1 - leaving_group

    packed = pack(leaving_group, query_rows, grad_rows, key_rows, value_rows)
    arrived = swapped(packed, "dp", far_bit)

    ids = doc_ids.reshape(group_count, STEPS, ROWS)
    leaving_ids = lax.dynamic_index_in_dim(ids, leaving_group[0], 0, keepdims=False)
    marks = jnp.concatenate(
        [
            jnp.pad(leaving_ids // 16, ((0, 8 - STEPS), (0, 0))),
            jnp.pad(leaving_ids % 16, ((0, 8 - STEPS), (0, 0))),
        ],
        axis=0,
    ).astype(jnp.bfloat16)
    arrived_marks = swapped(marks, "dp", far_bit)

    docs = jnp.pad(ids.astype(jnp.float32), ((0, 0), (0, 8 - STEPS), (0, 0)))
    wide = pl.BlockSpec((ROWS, width), lambda i, s: (s[0] * STEPS + i, 0))
    narrow = pl.BlockSpec((SLOT, kv_width), lambda i, s: (s[0], 0))
    held = attend(
        staying,
        docs,
        (query_rows, grad_rows, key_rows, value_rows),
        [pl.BlockSpec((1, 8, ROWS), lambda i, s: (s[0], 0, 0)), wide, wide, narrow, narrow],
        row_count,
        width,
        kv_width,
    )

    final = attend(
        leaving_group,
        arrived_marks,
        (arrived,) * 4,
        [
            pl.BlockSpec((16, ROWS), lambda i, s: (0, 0)),
            pl.BlockSpec((heads, ROWS, HEAD_DIM), lambda i, s: (0, i, 0)),
            pl.BlockSpec((heads, ROWS, HEAD_DIM), lambda i, s: (1, i, 0)),
            pl.BlockSpec((1, SLOT, HEAD_DIM), lambda i, s: (2 * heads, 0, 0)),
            pl.BlockSpec((1, SLOT, HEAD_DIM), lambda i, s: (2 * heads + 1, 0, 0)),
        ],
        row_count,
        width,
        kv_width,
        held=held,
    )
    return tuple(final)


def solution(mesh):
    return jax.shard_map(
        body,
        mesh=mesh,
        in_specs=(P("dp", "mp"), P("dp", "mp"), P("dp", "mp"), P("dp", "mp"), P("dp"), P("dp")),
        out_specs=(P("dp", "mp"), P("dp", "mp"), P("dp", "mp"), P("dp", "mp")),
        check_vma=False,
    )
```

time: 144 us -> 138 us (0.958)
  the two profiles are of different devices: /device:TPU:1 before, /device:TPU:40 now
where the time goes in v1:
time: 138 us
  waiting for transfers between devices  79.6 us (58%)
  Pallas kernels  39.8 us (29%)
  starting transfers between devices  16.7 us (12%)
  between operations  1.42 us (1%)
    ppermute x2, waiting for transfers between devices, swapped(): lax.ppermute(x, axis, [(i, i ^ 1 << bit) for i in range(lax.axis_size(axi...  79.6 us
    pallas_call x1, Pallas kernels, pack(): pl.pallas_call(pack_kernel, out_shape=jax.ShapeDtypeStruct((count, SLOT,...  31 us
    ppermute x2, starting transfers between devices, swapped(): lax.ppermute(x, axis, [(i, i ^ 1 << bit) for i in range(lax.axis_size(axi...  16.7 us
    pallas_call x2, Pallas kernels, attend(): pl.pallas_call(functools.partial(attend_kernel, received), out_shape=tupl...  8.8 us
  transfers between devices with their start and end apart: 2, of which 1 were waited for; matrix products, arithmetic and copies ran while one was open for 0% of the time, Pallas kernels for 3%

profile of v1, /device:TPU:40, one launch (start us, length us, event | category | flops | bytes accessed | tf_op | source)
XLA Modules:
  0.0 137.6 jit_solution(12547511886978219779)
XLA Ops:
  1.3 0.0 copy-start.4
  1.3 0.0 copy-start
  1.3 0.0 copy-start.1
  1.3 0.0 copy-start.2
  1.3 0.0 copy-start.3
  1.3 31.0 %pack_leaving.1 = bf16[10,384,128]{2,1,0:T(8,128)(2,1)} custom-call(s32[1]{0:T(128)} %copy.18.slot_ref, bf16[768,512]{1,0:T(8,128)(2,1)} %q_ref.3, bf16[768,512]{1,0:T(8,128)(2,1)} %g_ref.3, bf16[768,128]{1,0:T(8,128)(2,1)} %k_ref.3, bf16[768,128]{1,0:T(8,128)(2,1)} %v_ref.3), custom_call_target="tpu_custom_call" | custom-call | tf_op jit(solution)/shard_map/pack_leaving/pallas_call | solution.py:42
  32.3 14.8 %collective-permute-start.1 = (bf16[10,384,128]{2,1,0:T(8,128)(2,1)}, bf16[10,384,128]{2,1,0:T(8,128)(2,1)S(1)}, u32[]{:S(2)}, u32[]{:S(2)}) collective-permute-start(bf16[10,384,128]{2,1,0:T(8,128)(2,1)} %pack_leaving.1), channel_id=1, source_target_pairs={{0,256},{8,264},{16,272},{24,280},{32,288},{40,296},{48,304},{56,3... | collective-permute-start | bytes 2949128 | tf_op jit(solution)/shard_map/ppermute | solution.py:20
  47.1 0.0 copy-done.4
  47.2 1.9 %collective-permute-start = (bf16[16,128]{1,0:T(8,128)(2,1)S(1)}, bf16[16,128]{1,0:T(8,128)(2,1)S(1)}, u32[]{:S(2)}, u32[]{:S(2)}) collective-permute-start(bf16[16,128]{1,0:T(8,128)(2,1)S(1)} %fusion.2), channel_id=1, source_target_pairs={{0,256},{8,264},{16,272},{24,280},{32,288},{40,296},{48,304},{56,3... | collective-permute-start | bytes 12296 | tf_op jit(solution)/shard_map/ppermute | solution.py:20
  49.2 0.0 copy-done
  49.2 0.0 copy-done.1
  49.2 0.0 copy-done.2
  49.2 0.0 copy-done.3
  49.2 4.4 %attend_staying.1 = (bf16[768,512]{1,0:T(8,128)(2,1)}, bf16[768,512]{1,0:T(8,128)(2,1)}, bf16[768,128]{1,0:T(8,128)(2,1)}, bf16[768,128]{1,0:T(8,128)(2,1)}) custom-call(s32[1]{0:T(128)S(6)} %sub.10.slot_ref, f32[2,8,128]{2,1,0:T(8,128)S(1)} %pad.15.docs_ref, bf16[768,512]{1,0:T(8,128)(2,1)S(1)} %copy-done, bf16[768,512]{1,0:T(8,128)(2,1)S(1)} %copy-done.1, ...), custom_call_target="tpu_custom_call" | custom-call | flops 905969664 | bytes 4194304 | tf_op jit(solution)/shard_map/attend_staying/pallas_call | solution.py:141
  53.6 79.6 %collective-permute-done.docs_ref = bf16[16,128]{1,0:T(8,128)(2,1)S(1)} collective-permute-done((bf16[16,128]{1,0:T(8,128)(2,1)S(1)}, bf16[16,128]{1,0:T(8,128)(2,1)S(1)}, u32[]{:S(2)}, u32[]{:S(2)}) %collective-permute-start) | collective-permute-done | bytes 4128 | tf_op jit(solution)/shard_map/ppermute | solution.py:20
  133.1 0.0 collective-permute-done.1.q_ref.g_ref.k_ref.v_ref
  133.1 4.4 %attend_received.1 = (bf16[768,512]{1,0:T(8,128)(2,1)}, bf16[768,512]{1,0:T(8,128)(2,1)}, bf16[768,128]{1,0:T(8,128)(2,1)}, bf16[768,128]{1,0:T(8,128)(2,1)}) custom-call(s32[1]{0:T(128)} %copy.18.slot_ref, bf16[16,128]{1,0:T(8,128)(2,1)S(1)} %collective-permute-done.docs_ref, ...), custom_call_target="tpu_custom_call", output_to_operand_aliasing={{0}: (6, {}), {1}: (7, {}), {2}: (8, {}), {3}: (9, {})} | custom-call | flops 905969664 | bytes 4194304 | tf_op jit(solution)/shard_map/attend_received/pallas_call | solution.py:141
  (5 shorter events, 0.0 us)
Async XLA Ops:
  1.3 45.9 %copy-start.4 = (s32[768]{0:T(1024)S(1)}, s32[768]{0:T(1024)}, u32[]{:S(2)}) copy-start(s32[768]{0:T(1024)} %param.10) | copy-start | bytes 9220
  1.3 47.9 %copy-start = (bf16[768,512]{1,0:T(8,128)(2,1)S(1)}, bf16[768,512]{1,0:T(8,128)(2,1)}, u32[]{:S(2)}) copy-start(bf16[768,512]{1,0:T(8,128)(2,1)} %q_ref.3) | copy-start | bytes 2359300
  1.3 47.9 %copy-start.1 = (bf16[768,512]{1,0:T(8,128)(2,1)S(1)}, bf16[768,512]{1,0:T(8,128)(2,1)}, u32[]{:S(2)}) copy-start(bf16[768,512]{1,0:T(8,128)(2,1)} %g_ref.3) | copy-start | bytes 2359300
  1.3 47.9 %copy-start.2 = (bf16[768,128]{1,0:T(8,128)(2,1)S(1)}, bf16[768,128]{1,0:T(8,128)(2,1)}, u32[]{:S(2)}) copy-start(bf16[768,128]{1,0:T(8,128)(2,1)} %k_ref.3) | copy-start | bytes 589828
  1.3 47.9 %copy-start.3 = (bf16[768,128]{1,0:T(8,128)(2,1)S(1)}, bf16[768,128]{1,0:T(8,128)(2,1)}, u32[]{:S(2)}) copy-start(bf16[768,128]{1,0:T(8,128)(2,1)} %v_ref.3) | copy-start | bytes 589828
  32.3 100.8 %collective-permute-start.1 = (bf16[10,384,128]{2,1,0:T(8,128)(2,1)}, bf16[10,384,128]{2,1,0:T(8,128)(2,1)S(1)}, u32[]{:S(2)}, u32[]{:S(2)}) collective-permute-start(bf16[10,384,128]{2,1,0:T(8,128)(2,1)} %pack_leaving.1), channel_id=1, source_target_pairs={{0,256},{8,264},{16,272},{24,280},{32,288},{40,296},{48,304},{56,3... | collective-permute-start | bytes 2949128 | tf_op jit(solution)/shard_map/ppermute | solution.py:20
  47.2 85.9 %collective-permute-start = (bf16[16,128]{1,0:T(8,128)(2,1)S(1)}, bf16[16,128]{1,0:T(8,128)(2,1)S(1)}, u32[]{:S(2)}, u32[]{:S(2)}) collective-permute-start(bf16[16,128]{1,0:T(8,128)(2,1)S(1)} %fusion.2), channel_id=1, source_target_pairs={{0,256},{8,264},{16,272},{24,280},{32,288},{40,296},{48,304},{56,3... | collective-permute-start | bytes 12296 | tf_op jit(solution)/shard_map/ppermute | solution.py:20

commit v2 on v1

--- a/solution.py
+++ b/solution.py
@@ -20,20 +20,26 @@
     return lax.ppermute(x, axis, [(i, i ^ 1 << bit) for i in range(lax.axis_size(axis))])
 
 
-def pack_kernel(slot_ref, q_ref, g_ref, k_ref, v_ref, out_ref, sems):
+def pack_kernel(slot_ref, q_ref, g_ref, k_ref, v_ref, out_ref, held, sems, out_sems):
     heads = q_ref.shape[1] // HEAD_DIM
     base = pl.multiple_of(slot_ref[0] * SLOT, SLOT)
     rows = pl.ds(base, SLOT)
     parts = [q_ref.at[rows, pl.ds(h * HEAD_DIM, HEAD_DIM)] for h in range(heads)]
     parts += [g_ref.at[rows, pl.ds(h * HEAD_DIM, HEAD_DIM)] for h in range(heads)]
     parts += [k_ref.at[rows], v_ref.at[rows]]
-    copies = [
-        pltpu.make_async_copy(part, out_ref.at[i], sems.at[i]) for i, part in enumerate(parts)
+    loads = [
+        pltpu.make_async_copy(part, held.at[i], sems.at[i]) for i, part in enumerate(parts)
     ]
-    for copy in copies:
-        copy.start()
-    for copy in copies:
-        copy.wait()
+    stores = [
+        pltpu.make_async_copy(held.at[i], out_ref.at[i], out_sems.at[i]) for i in range(len(parts))
+    ]
+    for load in loads:
+        load.start()
+    for load, store in zip(loads, stores):
+        load.wait()
+        store.start()
+    for store in stores:
+        store.wait()
 
 
 def pack(slot, query, grad, key, value):
@@ -45,7 +51,11 @@
         in_specs=[pl.BlockSpec(memory_space=pltpu.SMEM)]
         + [pl.BlockSpec(memory_space=pltpu.HBM)] * 4,
         out_specs=pl.BlockSpec(memory_space=pl.ANY),
-        scratch_shapes=[pltpu.SemaphoreType.DMA((count,))],
+        scratch_shapes=[
+            pltpu.VMEM((count, SLOT, HEAD_DIM), query.dtype),
+            pltpu.SemaphoreType.DMA((count,)),
+            pltpu.SemaphoreType.DMA((count,)),
+        ],
         name="pack_leaving",
     )(slot, query, grad, key, value)
 

time: 138 us -> 109 us (0.79)
  Pallas kernels: 39.8 us -> 11.1 us
    pallas_call x1, Pallas kernels: 31 us -> 2.26 us  [pack(): pl.pallas_call(pack_kernel, out_shape=jax.ShapeDtypeStruct((count, SLOT,...]
  transfers between devices with their start and end apart: 2 -> 2, of which waited for: 1 -> 1; matrix products, arithmetic and copies ran while one was open for 0% -> 0% of each run, Pallas kernels for 3% -> 4%
where the time goes in v2:
time: 109 us
  waiting for transfers between devices  79.6 us (73%)
  starting transfers between devices  16.7 us (15%)
  Pallas kernels  11.1 us (10%)
  between operations  1.42 us (1%)
    ppermute x2, waiting for transfers between devices, swapped(): lax.ppermute(x, axis, [(i, i ^ 1 << bit) for i in range(lax.axis_size(axi...  79.6 us
    ppermute x2, starting transfers between devices, swapped(): lax.ppermute(x, axis, [(i, i ^ 1 << bit) for i in range(lax.axis_size(axi...  16.7 us
    pallas_call x2, Pallas kernels, attend(): pl.pallas_call(functools.partial(attend_kernel, received), out_shape=tupl...  8.8 us
    pallas_call x1, Pallas kernels, pack(): pl.pallas_call(pack_kernel, out_shape=jax.ShapeDtypeStruct((count, SLOT,...  2.26 us
  transfers between devices with their start and end apart: 2, of which 1 were waited for; matrix products, arithmetic and copies ran while one was open for 0% of the time, Pallas kernels for 4%

profile of v2, /device:TPU:40, one launch (start us, length us, event | category | flops | bytes accessed | tf_op | source)
XLA Modules:
  0.0 108.9 jit_solution(14748433628948587476)
XLA Ops:
  1.3 0.0 copy-start.4
  1.3 0.0 copy-start
  1.3 0.0 copy-start.1
  1.3 0.0 copy-start.2
  1.3 0.0 copy-start.3
  1.3 2.3 %pack_leaving.1 = bf16[10,384,128]{2,1,0:T(8,128)(2,1)} custom-call(s32[1]{0:T(128)} %copy.18.slot_ref, bf16[768,512]{1,0:T(8,128)(2,1)} %q_ref.3, bf16[768,512]{1,0:T(8,128)(2,1)} %g_ref.3, bf16[768,128]{1,0:T(8,128)(2,1)} %k_ref.3, bf16[768,128]{1,0:T(8,128)(2,1)} %v_ref.3), custom_call_target="tpu_custom_call" | custom-call | tf_op jit(solution)/shard_map/pack_leaving/pallas_call | solution.py:48
  3.6 14.8 %collective-permute-start.1 = (bf16[10,384,128]{2,1,0:T(8,128)(2,1)}, bf16[10,384,128]{2,1,0:T(8,128)(2,1)S(1)}, u32[]{:S(2)}, u32[]{:S(2)}) collective-permute-start(bf16[10,384,128]{2,1,0:T(8,128)(2,1)} %pack_leaving.1), channel_id=1, source_target_pairs={{0,256},{8,264},{16,272},{24,280},{32,288},{40,296},{48,304},{56,3... | collective-permute-start | bytes 2949128 | tf_op jit(solution)/shard_map/ppermute | solution.py:20
  18.4 0.0 copy-done.4
  18.5 1.9 %collective-permute-start = (bf16[16,128]{1,0:T(8,128)(2,1)S(1)}, bf16[16,128]{1,0:T(8,128)(2,1)S(1)}, u32[]{:S(2)}, u32[]{:S(2)}) collective-permute-start(bf16[16,128]{1,0:T(8,128)(2,1)S(1)} %fusion.2), channel_id=1, source_target_pairs={{0,256},{8,264},{16,272},{24,280},{32,288},{40,296},{48,304},{56,3... | collective-permute-start | bytes 12296 | tf_op jit(solution)/shard_map/ppermute | solution.py:20
  20.4 0.0 copy-done
  20.5 0.0 copy-done.1
  20.5 0.0 copy-done.2
  20.5 0.0 copy-done.3
  20.5 4.4 %attend_staying.1 = (bf16[768,512]{1,0:T(8,128)(2,1)}, bf16[768,512]{1,0:T(8,128)(2,1)}, bf16[768,128]{1,0:T(8,128)(2,1)}, bf16[768,128]{1,0:T(8,128)(2,1)}) custom-call(s32[1]{0:T(128)S(6)} %sub.10.slot_ref, f32[2,8,128]{2,1,0:T(8,128)S(1)} %pad.15.docs_ref, bf16[768,512]{1,0:T(8,128)(2,1)S(1)} %copy-done, bf16[768,512]{1,0:T(8,128)(2,1)S(1)} %copy-done.1, ...), custom_call_target="tpu_custom_call" | custom-call | flops 905969664 | bytes 4194304 | tf_op jit(solution)/shard_map/attend_staying/pallas_call | solution.py:151
  24.8 79.6 %collective-permute-done.docs_ref = bf16[16,128]{1,0:T(8,128)(2,1)S(1)} collective-permute-done((bf16[16,128]{1,0:T(8,128)(2,1)S(1)}, bf16[16,128]{1,0:T(8,128)(2,1)S(1)}, u32[]{:S(2)}, u32[]{:S(2)}) %collective-permute-start) | collective-permute-done | bytes 4128 | tf_op jit(solution)/shard_map/ppermute | solution.py:20
  104.4 0.0 collective-permute-done.1.q_ref.g_ref.k_ref.v_ref
  104.4 4.4 %attend_received.1 = (bf16[768,512]{1,0:T(8,128)(2,1)}, bf16[768,512]{1,0:T(8,128)(2,1)}, bf16[768,128]{1,0:T(8,128)(2,1)}, bf16[768,128]{1,0:T(8,128)(2,1)}) custom-call(s32[1]{0:T(128)} %copy.18.slot_ref, bf16[16,128]{1,0:T(8,128)(2,1)S(1)} %collective-permute-done.docs_ref, ...), custom_call_target="tpu_custom_call", output_to_operand_aliasing={{0}: (6, {}), {1}: (7, {}), {2}: (8, {}), {3}: (9, {})} | custom-call | flops 905969664 | bytes 4194304 | tf_op jit(solution)/shard_map/attend_received/pallas_call | solution.py:151
  (5 shorter events, 0.0 us)
Async XLA Ops:
  1.3 17.1 %copy-start.4 = (s32[768]{0:T(1024)S(1)}, s32[768]{0:T(1024)}, u32[]{:S(2)}) copy-start(s32[768]{0:T(1024)} %param.10) | copy-start | bytes 9220
  1.3 19.2 %copy-start = (bf16[768,512]{1,0:T(8,128)(2,1)S(1)}, bf16[768,512]{1,0:T(8,128)(2,1)}, u32[]{:S(2)}) copy-start(bf16[768,512]{1,0:T(8,128)(2,1)} %q_ref.3) | copy-start | bytes 2359300
  1.3 19.2 %copy-start.1 = (bf16[768,512]{1,0:T(8,128)(2,1)S(1)}, bf16[768,512]{1,0:T(8,128)(2,1)}, u32[]{:S(2)}) copy-start(bf16[768,512]{1,0:T(8,128)(2,1)} %g_ref.3) | copy-start | bytes 2359300
  1.3 19.2 %copy-start.2 = (bf16[768,128]{1,0:T(8,128)(2,1)S(1)}, bf16[768,128]{1,0:T(8,128)(2,1)}, u32[]{:S(2)}) copy-start(bf16[768,128]{1,0:T(8,128)(2,1)} %k_ref.3) | copy-start | bytes 589828
  1.3 19.2 %copy-start.3 = (bf16[768,128]{1,0:T(8,128)(2,1)S(1)}, bf16[768,128]{1,0:T(8,128)(2,1)}, u32[]{:S(2)}) copy-start(bf16[768,128]{1,0:T(8,128)(2,1)} %v_ref.3) | copy-start | bytes 589828
  3.6 100.8 %collective-permute-start.1 = (bf16[10,384,128]{2,1,0:T(8,128)(2,1)}, bf16[10,384,128]{2,1,0:T(8,128)(2,1)S(1)}, u32[]{:S(2)}, u32[]{:S(2)}) collective-permute-start(bf16[10,384,128]{2,1,0:T(8,128)(2,1)} %pack_leaving.1), channel_id=1, source_target_pairs={{0,256},{8,264},{16,272},{24,280},{32,288},{40,296},{48,304},{56,3... | collective-permute-start | bytes 2949128 | tf_op jit(solution)/shard_map/ppermute | solution.py:20
  18.5 85.9 %collective-permute-start = (bf16[16,128]{1,0:T(8,128)(2,1)S(1)}, bf16[16,128]{1,0:T(8,128)(2,1)S(1)}, u32[]{:S(2)}, u32[]{:S(2)}) collective-permute-start(bf16[16,128]{1,0:T(8,128)(2,1)S(1)} %fusion.2), channel_id=1, source_target_pairs={{0,256},{8,264},{16,272},{24,280},{32,288},{40,296},{48,304},{56,3... | collective-permute-start | bytes 12296 | tf_op jit(solution)/shard_map/ppermute | solution.py:20

commit v3 on v0

v3 whole, which is shorter than its diff:
```python
import functools

import jax
import jax.numpy as jnp
from jax import lax
from jax.experimental import pallas as pl
from jax.experimental.pallas import tpu as pltpu
from jax.sharding import PartitionSpec as P

HEAD_DIM = 128
SLOT = 384
LANES = 128
RUNS = SLOT // LANES
LOG2E = 1.4426950408889634
SCALING = HEAD_DIM ** (-0.5)
MASKED = -1e30 * LOG2E
OVER_LANES = (((1,), (1,)), ((), ()))
HBM = pl.BlockSpec(memory_space=pltpu.HBM)


def swapped(x, axis, bit):
    return lax.ppermute(x, axis, [(i, i ^ 1 << bit) for i in range(lax.axis_size(axis))])


def pack_kernel(heads, whole, slot_ref, *refs):
    if whole:
        *inputs, ids_ref, out_ref, ids, sems = refs
        ids_copy = pltpu.make_async_copy(ids_ref, ids, sems.at[sems.shape[0] - 1])
        ids_copy.start()
    else:
        *inputs, out_ref, sems = refs
    rows = pl.ds(pl.multiple_of(slot_ref[0] * SLOT, SLOT), SLOT)
    parts = [
        ref.at[rows, pl.ds(h * HEAD_DIM, HEAD_DIM)] for ref in inputs[:2] for h in heads
    ]
    parts += [ref.at[rows] for ref in inputs[2:]]
    copies = [
        pltpu.make_async_copy(part, out_ref.at[pl.ds(i * SLOT, SLOT)], sems.at[i])
        for i, part in enumerate(parts)
    ]
    for copy in copies:
        copy.start()
    if whole:
        ids_copy.wait()
        lines = [
            ids[j * LANES : (j + 1) * LANES].reshape(1, LANES) for j in range(ids.shape[0] // LANES)
        ]
        here = jnp.concatenate(lines[:RUNS], axis=0)
        for group in range(1, len(lines) // RUNS):
            other = jnp.concatenate(lines[group * RUNS : (group + 1) * RUNS], axis=0)
            here = jnp.where(slot_ref[0] == group, other, here)
        blank = jnp.zeros((8 - RUNS, LANES), jnp.int32)
        marks = jnp.concatenate([here >> 4, blank, here & 15, blank], axis=0)
        out_ref[len(parts) * SLOT :, :] = marks.astype(jnp.float32).astype(out_ref.dtype)
    for copy in copies:
        copy.wait()


def pack(slot, heads, query, grad, pair=(), doc_ids=None):
    whole = doc_ids is not None
    count = 2 * len(heads) + len(pair)
    inputs = (query, grad, *pair) + ((doc_ids,) if whole else ())
    inputs = [pltpu.with_memory_space_constraint(x, pltpu.HBM) for x in inputs]
    packed = jax.ShapeDtypeStruct((count * SLOT + 16 * whole, HEAD_DIM), query.dtype)
    scratch = [pltpu.VMEM(doc_ids.shape, jnp.int32)] if whole else []
    return pl.pallas_call(
        functools.partial(pack_kernel, heads, whole),
        out_shape=packed,
        in_specs=[pl.BlockSpec(memory_space=pltpu.SMEM)] + [HBM] * len(inputs),
        out_specs=pl.BlockSpec(memory_space=pltpu.VMEM),
        scratch_shapes=scratch + [pltpu.SemaphoreType.DMA((count + whole,))],
        compiler_params=pltpu.CompilerParams(vmem_limit_bytes=4 * 1024 * 1024),
        name="pack_" + "_".join(str(h) for h in heads),
    )(slot, *inputs)


def attend_head(ids, q, g, keys, values, keys_t, values_t):
    scores = lax.dot_general(keys, q, OVER_LANES, preferred_element_type=jnp.float32)
    dprobs = lax.dot_general(values, g, OVER_LANES, preferred_element_type=jnp.float32)
    ids_t = ids.T
    key_ids = jnp.concatenate([ids_t[:, j : j + 1] for j in range(RUNS)], axis=0)
    row_ids = jnp.concatenate([ids[j : j + 1, :] for j in range(RUNS)], axis=1)
    key_places = lax.broadcasted_iota(jnp.int32, (SLOT, SLOT), 0)
    row_places = lax.broadcasted_iota(jnp.int32, (SLOT, SLOT), 1)
    allowed = (key_ids == row_ids) & (key_places <= row_places)
    scores = jnp.where(allowed, scores * (SCALING * LOG2E), MASKED)
    weights = jnp.exp2(scores - jnp.max(scores, axis=0, keepdims=True))
    probs = weights * (1.0 / jnp.sum(weights, axis=0, keepdims=True))
    inner_sum = jnp.sum(probs * dprobs, axis=0, keepdims=True)
    probs16 = probs.astype(jnp.bfloat16)
    dscores = (probs * (dprobs - inner_sum)).astype(jnp.bfloat16)
    dv = jnp.dot(probs16, g, preferred_element_type=jnp.float32)
    dk = jnp.dot(dscores, q, preferred_element_type=jnp.float32)
    out_t = jnp.dot(values_t, probs16, preferred_element_type=jnp.float32)
    dq_t = jnp.dot(keys_t, dscores, preferred_element_type=jnp.float32) * SCALING
    return out_t.T.astype(jnp.bfloat16), dq_t.T.astype(jnp.bfloat16), dk, dv


def attend_kernel(count, first, last, held, slot_ref, marks_ref, q_ref, g_ref, k_ref, v_ref, *rest):
    if not first:
        dk_in, dv_in, *rest = rest
    o_ref, dq_ref, dk_ref, dv_ref, keys_t, values_t, dk_sum, dv_sum = rest[held:]
    index = pl.program_id(0)

    @pl.when(index == 0)
    def _():
        keys_t[...] = k_ref[...].T
        values_t[...] = v_ref[...].T
        dk_sum[...] = jnp.zeros_like(dk_sum) if first else dk_in[...]
        dv_sum[...] = jnp.zeros_like(dv_sum) if first else dv_in[...]

    marks = marks_ref[...].astype(jnp.float32)
    ids = marks[:8] * 16.0 + marks[8:]
    out, dq, dk, dv = attend_head(
        ids, q_ref[...], g_ref[...], k_ref[...], v_ref[...], keys_t[...], values_t[...]
    )
    o_ref[...] = out
    dq_ref[...] = dq
    dk_sum[...] += dk
    dv_sum[...] += dv

    @pl.when(index == count - 1)
    def _():
        if last:
            dk_ref[...] = (dk_sum[...] * SCALING).astype(jnp.bfloat16)
            dv_ref[...] = dv_sum[...].astype(jnp.bfloat16)
        else:
            dk_ref[...] = dk_sum[...]
            dv_ref[...] = dv_sum[...]


def attend(slot, heads, inputs, places, row_count, width, partial=None, held=(), last=True):
    def block(place, rows=SLOT):
        return pl.BlockSpec((rows, HEAD_DIM), place)

    first = partial is None
    wide = block(lambda h, s: (s[0], h + heads[0]))
    whole = block(lambda h, s: (0, 0))
    narrow = block(lambda h, s: (s[0], 0)) if last else whole
    in_specs = [block(places[0], 16)] + [block(place) for place in places[1:]]
    in_specs += [whole, whole] * (not first) + [pl.BlockSpec(memory_space=pl.ANY)] * len(held)
    sum_shape = jax.ShapeDtypeStruct((SLOT, HEAD_DIM), jnp.float32)
    wide_shape = jax.ShapeDtypeStruct((row_count, width), jnp.bfloat16)
    narrow_shape = jax.ShapeDtypeStruct((row_count, HEAD_DIM), jnp.bfloat16)
    begin = 1 + len(inputs) + 2 * (not first)
    return pl.pallas_call(
        functools.partial(attend_kernel, len(heads), first, last, len(held)),
        out_shape=(wide_shape, wide_shape) + ((narrow_shape,) * 2 if last else (sum_shape,) * 2),
        grid_spec=pltpu.PrefetchScalarGridSpec(
            num_scalar_prefetch=1,
            grid=(len(heads),),
            in_specs=in_specs,
            out_specs=(wide, wide, narrow, narrow),
            scratch_shapes=[pltpu.VMEM((HEAD_DIM, SLOT), jnp.bfloat16)] * 2
            + [pltpu.VMEM((SLOT, HEAD_DIM), jnp.float32)] * 2,
        ),
        input_output_aliases={begin + i: i for i in range(len(held))},
        compiler_params=pltpu.CompilerParams(vmem_limit_bytes=16 * 1024 * 1024),
        cost_estimate=pl.CostEstimate(
            flops=12 * len(heads) * SLOT * SLOT * HEAD_DIM,
            bytes_accessed=(4 * len(heads) + 4) * SLOT * HEAD_DIM * 2,
            transcendentals=SLOT * SLOT * len(heads),
        ),
        name="attend_" + "_".join(str(h) for h in heads),
    )(slot, *inputs, *(() if first else partial), *held)


def body(query_rows, key_rows, value_rows, grad_rows, doc_ids, leaving_group):
    row_count, width = query_rows.shape
    heads = tuple(range(width // HEAD_DIM))
    early, late = heads[:-1], heads[-1:]
    group_count = row_count // SLOT
    far_bit = lax.axis_size("dp").bit_length() - 2

    most = pack(leaving_group, early, query_rows, grad_rows, (key_rows, value_rows), doc_ids)
    most, query_rows, grad_rows = lax.optimization_barrier((most, query_rows, grad_rows))
    most = swapped(most, "dp", far_bit)
    rest = pack(leaving_group, late, query_rows, grad_rows)
    rest = swapped(rest, "dp", far_bit)

    ids = jnp.pad(doc_ids.reshape(group_count, RUNS, LANES), ((0, 0), (0, 8 - RUNS), (0, 0)))
    marks = jnp.concatenate([ids // 16, ids % 16], axis=1).astype(jnp.bfloat16)
    staying = group_count - 1 - leaving_group

    held = attend(
        staying,
        heads,
        (marks.reshape(group_count * 16, LANES), query_rows, grad_rows, key_rows, value_rows),
        (
            lambda h, s: (s[0], 0),
            lambda h, s: (s[0], h),
            lambda h, s: (s[0], h),
            lambda h, s: (s[0], 0),
            lambda h, s: (s[0], 0),
        ),
        row_count,
        width,
    )

    pair_at = 2 * len(early)
    marks_at = (pair_at + 2) * (SLOT // 16)

    def marks_place(h, s):
        return (marks_at, 0)

    pair_places = (lambda h, s: (pair_at, 0), lambda h, s: (pair_at + 1, 0))
    out, dq, *partial = attend(
        leaving_group,
        early,
        (most, most, most, most, most),
        (
            marks_place,
            lambda h, s: (h, 0),
            lambda h, s: (h + len(early), 0),
            *pair_places,
        ),
        row_count,
        width,
        held=held[:2],
        last=False,
    )
    return tuple(
        attend(
            leaving_group,
            late,
            (most, rest, rest, most, most),
            (
                marks_place,
                lambda h, s: (0, 0),
                lambda h, s: (1, 0),
                *pair_places,
            ),
            row_count,
            width,
            partial=partial,
            held=(out, dq, *held[2:]),
        )
    )


def solution(mesh):
    return jax.shard_map(
        body,
        mesh=mesh,
        in_specs=(P("dp", "mp"), P("dp", "mp"), P("dp", "mp"), P("dp", "mp"), P("dp"), P("dp")),
        out_specs=(P("dp", "mp"), P("dp", "mp"), P("dp", "mp"), P("dp", "mp")),
        check_vma=False,
    )
```

time: 144 us -> 106 us (0.74)
  the two profiles are of different devices: /device:TPU:1 before, /device:TPU:36 now
where the time goes in v3:
time: 106 us
  waiting for transfers between devices  72.5 us (68%)
  starting transfers between devices  16.9 us (16%)
  Pallas kernels  13.8 us (13%)
  between operations  1.41 us (1%)
    ppermute x2, waiting for transfers between devices, swapped(): lax.ppermute(x, axis, [(i, i ^ 1 << bit) for i in range(lax.axis_size(axi...  72.5 us
    ppermute x2, starting transfers between devices, swapped(): lax.ppermute(x, axis, [(i, i ^ 1 << bit) for i in range(lax.axis_size(axi...  16.9 us
    pallas_call x3, Pallas kernels, attend(): pl.pallas_call(functools.partial(attend_kernel, len(heads), first, last,...  10.9 us
    pallas_call x2, Pallas kernels, pack(): pl.pallas_call(functools.partial(pack_kernel, heads, whole), out_shape=pa...  2.96 us
  transfers between devices with their start and end apart: 2, of which 1 were waited for; matrix products, arithmetic and copies ran while one was open for 0% of the time, Pallas kernels for 10%

profile of v3, /device:TPU:36, one launch (start us, length us, event | category | flops | bytes accessed | tf_op | source)
XLA Modules:
  0.0 105.6 jit_solution(17555674862020804593)
XLA Ops:
  1.3 0.0 copy-start.4
  1.3 1.3 %pack_0_1_2.1 = bf16[3088,128]{1,0:T(8,128)(2,1)S(1)} custom-call(s32[1]{0:T(128)S(6)} %copy.22.slot_ref, bf16[768,512]{1,0:T(8,128)(2,1)} %q_ref, bf16[768,512]{1,0:T(8,128)(2,1)} %g_ref, bf16[768,128]{1,0:T(8,128)(2,1)} %k_ref.1, bf16[768,128]{1,0:T(8,128)(2,1)} %v_ref.1, s32[768]{0:T(1024)} %refs_4_.1), custom_call_target="tpu_custom_call" | custom-call | tf_op jit(solution)/shard_map/pack_0_1_2/pallas_call | solution.py:66
  2.6 0.0 copy-start
  2.6 0.0 copy-start.1
  2.6 0.0 copy-start.2
  2.7 15.0 %collective-permute-start = (bf16[3088,128]{1,0:T(8,128)(2,1)S(1)}, bf16[3088,128]{1,0:T(8,128)(2,1)S(1)}, u32[]{:S(2)}, u32[]{:S(2)}) collective-permute-start(bf16[3088,128]{1,0:T(8,128)(2,1)S(1)} %pack_0_1_2.1), channel_id=1, source_target_pairs={{0,256},{8,264},{16,272},{24,280},{32,288},{40,296},{48,304},{56,3... | collective-permute-start | bytes 2371592 | tf_op jit(solution)/shard_map/ppermute | solution.py:22
  17.6 1.6 %pack_3.1 = bf16[768,128]{1,0:T(8,128)(2,1)} custom-call(s32[1]{0:T(128)S(6)} %copy.22.slot_ref, bf16[768,512]{1,0:T(8,128)(2,1)} %q_ref, bf16[768,512]{1,0:T(8,128)(2,1)} %g_ref), custom_call_target="tpu_custom_call" | custom-call | tf_op jit(solution)/shard_map/pack_3/pallas_call | solution.py:66
  19.3 1.9 %collective-permute-start.1 = (bf16[768,128]{1,0:T(8,128)(2,1)}, bf16[768,128]{1,0:T(8,128)(2,1)S(1)}, u32[]{:S(2)}, u32[]{:S(2)}) collective-permute-start(bf16[768,128]{1,0:T(8,128)(2,1)} %pack_3.1), channel_id=1, source_target_pairs={{0,256},{8,264},{16,272},{24,280},{32,288},{40,296},{48,304},{56,3... | collective-permute-start | bytes 589832 | tf_op jit(solution)/shard_map/ppermute | solution.py:22
  21.2 0.0 copy-done.4
  21.3 0.0 copy-done
  21.3 0.0 copy-done.1
  21.3 0.0 copy-done.2
  21.3 0.0 copy-start.3
  21.3 0.9 copy-done.3
  22.2 5.3 %attend_0_1_2_3.1 = (bf16[768,512]{1,0:T(8,128)(2,1)}, bf16[768,512]{1,0:T(8,128)(2,1)}, bf16[768,128]{1,0:T(8,128)(2,1)}, bf16[768,128]{1,0:T(8,128)(2,1)}) custom-call(s32[1]{0:T(128)S(6)} %sub.9.slot_ref, bf16[32,128]{1,0:T(8,128)(2,1)S(1)} %bitcast.1, bf16[768,512]{1,0:T(8,128)(2,1)S(1)} %copy-done, bf16[768,512]{1,0:T(8,128)(2,1)S(1)} %copy-done.1, ...), custom_call_target="tpu_custom_call" | custom-call | flops 905969664 | bytes 1966080 | tf_op jit(solution)/shard_map/attend_0_1_2_3/pallas_call | solution.py:146
  27.5 72.5 %collective-permute-done.marks_ref.q_ref.g_ref.k_ref.v_ref = bf16[3088,128]{1,0:T(8,128)(2,1)S(1)} collective-permute-done((bf16[3088,128]{1,0:T(8,128)(2,1)S(1)}, bf16[3088,128]{1,0:T(8,128)(2,1)S(1)}, u32[]{:S(2)}, u32[]{:S(2)}) %collective-permute-start) | collective-permute-done | bytes 790560 | tf_op jit(solution)/shard_map/ppermute | solution.py:22
  100.0 3.9 %attend_0_1_2.1 = (bf16[768,512]{1,0:T(8,128)(2,1)}, bf16[768,512]{1,0:T(8,128)(2,1)}, f32[384,128]{1,0:T(8,128)S(1)}, f32[384,128]{1,0:T(8,128)S(1)}) custom-call(s32[1]{0:T(128)S(6)} %copy.22.slot_ref, bf16[3088,128]{1,0:T(8,128)(2,1)S(1)} %collective-permute-done.marks_ref.q_ref.g_ref.k_ref.v_ref, ...), custom_call_target="tpu_custom_call", output_to_operand_aliasing={{0}: (6, {}), {1}: (7, {})} | custom-call | flops 679477248 | bytes 1572864 | tf_op jit(solution)/shard_map/attend_0_1_2/pallas_call | solution.py:146
  103.9 0.0 collective-permute-done.1.q_ref.g_ref
  103.9 1.7 %attend_3.1 = (bf16[768,512]{1,0:T(8,128)(2,1)}, bf16[768,512]{1,0:T(8,128)(2,1)}, bf16[768,128]{1,0:T(8,128)(2,1)}, bf16[768,128]{1,0:T(8,128)(2,1)}) custom-call(s32[1]{0:T(128)S(6)} %copy.22.slot_ref, ...), custom_call_target="tpu_custom_call", output_to_operand_aliasing={{0}: (8, {}), {1}: (9, {}), {2}: (10, {}), {3}: (11, {})} | custom-call | flops 226492416 | bytes 786432 | tf_op jit(solution)/shard_map/attend_3/pallas_call | solution.py:146
  (3 shorter events, 0.0 us)
Async XLA Ops:
  1.3 19.9 %copy-start.4 = (s32[768]{0:T(1024)S(1)}, s32[768]{0:T(1024)}, u32[]{:S(2)}) copy-start(s32[768]{0:T(1024)} %refs_4_.1) | copy-start | bytes 9220
  2.6 18.6 %copy-start = (bf16[768,512]{1,0:T(8,128)(2,1)S(1)}, bf16[768,512]{1,0:T(8,128)(2,1)}, u32[]{:S(2)}) copy-start(bf16[768,512]{1,0:T(8,128)(2,1)} %q_ref) | copy-start | bytes 2359300
  2.6 18.6 %copy-start.1 = (bf16[768,512]{1,0:T(8,128)(2,1)S(1)}, bf16[768,512]{1,0:T(8,128)(2,1)}, u32[]{:S(2)}) copy-start(bf16[768,512]{1,0:T(8,128)(2,1)} %g_ref) | copy-start | bytes 2359300
  2.6 18.6 %copy-start.2 = (bf16[768,128]{1,0:T(8,128)(2,1)S(1)}, bf16[768,128]{1,0:T(8,128)(2,1)}, u32[]{:S(2)}) copy-start(bf16[768,128]{1,0:T(8,128)(2,1)} %k_ref.1) | copy-start | bytes 589828
  2.7 97.4 %collective-permute-start = (bf16[3088,128]{1,0:T(8,128)(2,1)S(1)}, bf16[3088,128]{1,0:T(8,128)(2,1)S(1)}, u32[]{:S(2)}, u32[]{:S(2)}) collective-permute-start(bf16[3088,128]{1,0:T(8,128)(2,1)S(1)} %pack_0_1_2.1), channel_id=1, source_target_pairs={{0,256},{8,264},{16,272},{24,280},{32,288},{40,296},{48,304},{56,3... | collective-permute-start | bytes 2371592 | tf_op jit(solution)/shard_map/ppermute | solution.py:22
  19.3 84.6 %collective-permute-start.1 = (bf16[768,128]{1,0:T(8,128)(2,1)}, bf16[768,128]{1,0:T(8,128)(2,1)S(1)}, u32[]{:S(2)}, u32[]{:S(2)}) collective-permute-start(bf16[768,128]{1,0:T(8,128)(2,1)} %pack_3.1), channel_id=1, source_target_pairs={{0,256},{8,264},{16,272},{24,280},{32,288},{40,296},{48,304},{56,3... | collective-permute-start | bytes 589832 | tf_op jit(solution)/shard_map/ppermute | solution.py:22
  21.3 0.9 copy-start.3

commit v4 on v3

--- a/solution.py
+++ b/solution.py
@@ -15,6 +15,8 @@
 SCALING = HEAD_DIM ** (-0.5)
 MASKED = -1e30 * LOG2E
 OVER_LANES = (((1,), (1,)), ((), ()))
+RING = 16
+YIELDING = (5, 7)
 HBM = pl.BlockSpec(memory_space=pltpu.HBM)
 
 
@@ -38,9 +40,20 @@
         pltpu.make_async_copy(part, out_ref.at[pl.ds(i * SLOT, SLOT)], sems.at[i])
         for i, part in enumerate(parts)
     ]
-    for copy in copies:
-        copy.start()
     if whole:
+        place = lax.axis_index("dp") * RING // lax.axis_size("dp")
+        yields = functools.reduce(jnp.logical_or, [place == z for z in YIELDING])
+        half = len(copies) // 2
+        for copy in copies[:half]:
+            copy.start()
+
+        @pl.when(yields)
+        def _():
+            for copy in copies[:half]:
+                copy.wait()
+
+        for copy in copies[half:]:
+            copy.start()
         ids_copy.wait()
         lines = [
             ids[j * LANES : (j + 1) * LANES].reshape(1, LANES) for j in range(ids.shape[0] // LANES)
@@ -52,8 +65,19 @@
         blank = jnp.zeros((8 - RUNS, LANES), jnp.int32)
         marks = jnp.concatenate([here >> 4, blank, here & 15, blank], axis=0)
         out_ref[len(parts) * SLOT :, :] = marks.astype(jnp.float32).astype(out_ref.dtype)
-    for copy in copies:
-        copy.wait()
+
+        @pl.when(jnp.logical_not(yields))
+        def _():
+            for copy in copies[:half]:
+                copy.wait()
+
+        for copy in copies[half:]:
+            copy.wait()
+    else:
+        for copy in copies:
+            copy.start()
+        for copy in copies:
+            copy.wait()
 
 
 def pack(slot, heads, query, grad, pair=(), doc_ids=None):

time: 106 us -> 104 us (0.981)
  the two profiles are of different devices: /device:TPU:36 before, /device:TPU:232 now
where the time goes in v4:
time: 104 us
  waiting for transfers between devices  71.9 us (69%)
  Pallas kernels  14.7 us (14%)
  starting transfers between devices  14.7 us (14%)
  between operations  1.41 us (1%)
    ppermute x2, waiting for transfers between devices, swapped(): lax.ppermute(x, axis, [(i, i ^ 1 << bit) for i in range(lax.axis_size(axi...  71.9 us
    ppermute x2, starting transfers between devices, swapped(): lax.ppermute(x, axis, [(i, i ^ 1 << bit) for i in range(lax.axis_size(axi...  14.7 us
    pallas_call x3, Pallas kernels, attend(): pl.pallas_call(functools.partial(attend_kernel, len(heads), first, last,...  10.9 us
    pallas_call x2, Pallas kernels, pack(): pl.pallas_call(functools.partial(pack_kernel, heads, whole), out_shape=pa...  3.82 us
  transfers between devices with their start and end apart: 2, of which 2 were waited for; matrix products, arithmetic and copies ran while one was open for 0% of the time, Pallas kernels for 10%

profile of v4, /device:TPU:232, one launch (start us, length us, event | category | flops | bytes accessed | tf_op | source)
XLA Modules:
  0.0 103.7 jit_solution(11205542989297515041)
XLA Ops:
  1.3 0.0 copy-start.4
  1.3 2.2 %pack_0_1_2.1 = bf16[3088,128]{1,0:T(8,128)(2,1)S(1)} custom-call(s32[1]{0:T(128)S(6)} %copy.22.slot_ref, bf16[768,512]{1,0:T(8,128)(2,1)} %q_ref, bf16[768,512]{1,0:T(8,128)(2,1)} %g_ref, bf16[768,128]{1,0:T(8,128)(2,1)} %k_ref.1, bf16[768,128]{1,0:T(8,128)(2,1)} %v_ref.1, s32[768]{0:T(1024)} %refs_4_.1), custom_call_target="tpu_custom_call" | custom-call | tf_op jit(solution)/shard_map/pack_0_1_2/pallas_call | solution.py:90
  3.5 0.0 copy-start
  3.5 0.0 copy-start.1
  3.5 0.0 copy-start.2
  3.5 7.5 %collective-permute-start = (bf16[3088,128]{1,0:T(8,128)(2,1)S(1)}, bf16[3088,128]{1,0:T(8,128)(2,1)S(1)}, u32[]{:S(2)}, u32[]{:S(2)}) collective-permute-start(bf16[3088,128]{1,0:T(8,128)(2,1)S(1)} %pack_0_1_2.1), channel_id=1, source_target_pairs={{0,256},{8,264},{16,272},{24,280},{32,288},{40,296},{48,304},{56,3... | collective-permute-start | bytes 2371592 | tf_op jit(solution)/shard_map/ppermute | solution.py:24
  11.0 1.6 %pack_3.1 = bf16[768,128]{1,0:T(8,128)(2,1)} custom-call(s32[1]{0:T(128)S(6)} %copy.22.slot_ref, bf16[768,512]{1,0:T(8,128)(2,1)} %q_ref, bf16[768,512]{1,0:T(8,128)(2,1)} %g_ref), custom_call_target="tpu_custom_call" | custom-call | tf_op jit(solution)/shard_map/pack_3/pallas_call | solution.py:90
  12.7 7.2 %collective-permute-start.1 = (bf16[768,128]{1,0:T(8,128)(2,1)}, bf16[768,128]{1,0:T(8,128)(2,1)S(1)}, u32[]{:S(2)}, u32[]{:S(2)}) collective-permute-start(bf16[768,128]{1,0:T(8,128)(2,1)} %pack_3.1), channel_id=1, source_target_pairs={{0,256},{8,264},{16,272},{24,280},{32,288},{40,296},{48,304},{56,3... | collective-permute-start | bytes 589832 | tf_op jit(solution)/shard_map/ppermute | solution.py:24
  19.9 0.0 copy-done.4
  19.9 0.0 copy-done
  19.9 0.0 copy-done.1
  19.9 0.0 copy-done.2
  20.0 0.0 copy-start.3
  20.0 0.9 copy-done.3
  20.9 5.3 %attend_0_1_2_3.1 = (bf16[768,512]{1,0:T(8,128)(2,1)}, bf16[768,512]{1,0:T(8,128)(2,1)}, bf16[768,128]{1,0:T(8,128)(2,1)}, bf16[768,128]{1,0:T(8,128)(2,1)}) custom-call(s32[1]{0:T(128)S(6)} %sub.9.slot_ref, bf16[32,128]{1,0:T(8,128)(2,1)S(1)} %bitcast.1, bf16[768,512]{1,0:T(8,128)(2,1)S(1)} %copy-done, bf16[768,512]{1,0:T(8,128)(2,1)S(1)} %copy-done.1, ...), custom_call_target="tpu_custom_call" | custom-call | flops 905969664 | bytes 1966080 | tf_op jit(solution)/shard_map/attend_0_1_2_3/pallas_call | solution.py:170
  26.2 71.6 %collective-permute-done.marks_ref.q_ref.g_ref.k_ref.v_ref = bf16[3088,128]{1,0:T(8,128)(2,1)S(1)} collective-permute-done((bf16[3088,128]{1,0:T(8,128)(2,1)S(1)}, bf16[3088,128]{1,0:T(8,128)(2,1)S(1)}, u32[]{:S(2)}, u32[]{:S(2)}) %collective-permute-start) | collective-permute-done | bytes 790560 | tf_op jit(solution)/shard_map/ppermute | solution.py:24
  97.8 3.9 %attend_0_1_2.1 = (bf16[768,512]{1,0:T(8,128)(2,1)}, bf16[768,512]{1,0:T(8,128)(2,1)}, f32[384,128]{1,0:T(8,128)S(1)}, f32[384,128]{1,0:T(8,128)S(1)}) custom-call(s32[1]{0:T(128)S(6)} %copy.22.slot_ref, bf16[3088,128]{1,0:T(8,128)(2,1)S(1)} %collective-permute-done.marks_ref.q_ref.g_ref.k_ref.v_ref, ...), custom_call_target="tpu_custom_call", output_to_operand_aliasing={{0}: (6, {}), {1}: (7, {})} | custom-call | flops 679477248 | bytes 1572864 | tf_op jit(solution)/shard_map/attend_0_1_2/pallas_call | solution.py:170
  101.7 0.3 collective-permute-done.1.q_ref.g_ref
  102.0 1.7 %attend_3.1 = (bf16[768,512]{1,0:T(8,128)(2,1)}, bf16[768,512]{1,0:T(8,128)(2,1)}, bf16[768,128]{1,0:T(8,128)(2,1)}, bf16[768,128]{1,0:T(8,128)(2,1)}) custom-call(s32[1]{0:T(128)S(6)} %copy.22.slot_ref, ...), custom_call_target="tpu_custom_call", output_to_operand_aliasing={{0}: (8, {}), {1}: (9, {}), {2}: (10, {}), {3}: (11, {})} | custom-call | flops 226492416 | bytes 786432 | tf_op jit(solution)/shard_map/attend_3/pallas_call | solution.py:170
  (3 shorter events, 0.0 us)
Async XLA Ops:
  1.3 18.6 %copy-start.4 = (s32[768]{0:T(1024)S(1)}, s32[768]{0:T(1024)}, u32[]{:S(2)}) copy-start(s32[768]{0:T(1024)} %refs_4_.1) | copy-start | bytes 9220
  3.5 16.4 %copy-start = (bf16[768,512]{1,0:T(8,128)(2,1)S(1)}, bf16[768,512]{1,0:T(8,128)(2,1)}, u32[]{:S(2)}) copy-start(bf16[768,512]{1,0:T(8,128)(2,1)} %q_ref) | copy-start | bytes 2359300
  3.5 16.4 %copy-start.1 = (bf16[768,512]{1,0:T(8,128)(2,1)S(1)}, bf16[768,512]{1,0:T(8,128)(2,1)}, u32[]{:S(2)}) copy-start(bf16[768,512]{1,0:T(8,128)(2,1)} %g_ref) | copy-start | bytes 2359300
  3.5 16.4 %copy-start.2 = (bf16[768,128]{1,0:T(8,128)(2,1)S(1)}, bf16[768,128]{1,0:T(8,128)(2,1)}, u32[]{:S(2)}) copy-start(bf16[768,128]{1,0:T(8,128)(2,1)} %k_ref.1) | copy-start | bytes 589828
  3.5 94.3 %collective-permute-start = (bf16[3088,128]{1,0:T(8,128)(2,1)S(1)}, bf16[3088,128]{1,0:T(8,128)(2,1)S(1)}, u32[]{:S(2)}, u32[]{:S(2)}) collective-permute-start(bf16[3088,128]{1,0:T(8,128)(2,1)S(1)} %pack_0_1_2.1), channel_id=1, source_target_pairs={{0,256},{8,264},{16,272},{24,280},{32,288},{40,296},{48,304},{56,3... | collective-permute-start | bytes 2371592 | tf_op jit(solution)/shard_map/ppermute | solution.py:24
  12.7 89.3 %collective-permute-start.1 = (bf16[768,128]{1,0:T(8,128)(2,1)}, bf16[768,128]{1,0:T(8,128)(2,1)S(1)}, u32[]{:S(2)}, u32[]{:S(2)}) collective-permute-start(bf16[768,128]{1,0:T(8,128)(2,1)} %pack_3.1), channel_id=1, source_target_pairs={{0,256},{8,264},{16,272},{24,280},{32,288},{40,296},{48,304},{56,3... | collective-permute-start | bytes 589832 | tf_op jit(solution)/shard_map/ppermute | solution.py:24
  20.0 0.9 copy-start.3

commit v5 on v4

--- a/solution.py
+++ b/solution.py
@@ -22,6 +22,10 @@
 
 def swapped(x, axis, bit):
     return lax.ppermute(x, axis, [(i, i ^ 1 << bit) for i in range(lax.axis_size(axis))])
+
+
+def in_hbm(arrays):
+    return [pltpu.with_memory_space_constraint(x, pltpu.HBM) for x in arrays]
 
 
 def pack_kernel(heads, whole, slot_ref, *refs):
@@ -84,7 +88,7 @@
     whole = doc_ids is not None
     count = 2 * len(heads) + len(pair)
     inputs = (query, grad, *pair) + ((doc_ids,) if whole else ())
-    inputs = [pltpu.with_memory_space_constraint(x, pltpu.HBM) for x in inputs]
+    inputs = in_hbm(inputs)
     packed = jax.ShapeDtypeStruct((count * SLOT + 16 * whole, HEAD_DIM), query.dtype)
     scratch = [pltpu.VMEM(doc_ids.shape, jnp.int32)] if whole else []
     return pl.pallas_call(
@@ -98,7 +102,7 @@
     )(slot, *inputs)
 
 
-def attend_head(ids, q, g, keys, values, keys_t, values_t):
+def attend_weights(ids, q, g, keys, values):
     scores = lax.dot_general(keys, q, OVER_LANES, preferred_element_type=jnp.float32)
     dprobs = lax.dot_general(values, g, OVER_LANES, preferred_element_type=jnp.float32)
     ids_t = ids.T
@@ -112,7 +116,11 @@
     probs = weights * (1.0 / jnp.sum(weights, axis=0, keepdims=True))
     inner_sum = jnp.sum(probs * dprobs, axis=0, keepdims=True)
     probs16 = probs.astype(jnp.bfloat16)
-    dscores = (probs * (dprobs - inner_sum)).astype(jnp.bfloat16)
+    return probs16, (probs * (dprobs - inner_sum)).astype(jnp.bfloat16)
+
+
+def attend_head(ids, q, g, keys, values, keys_t, values_t):
+    probs16, dscores = attend_weights(ids, q, g, keys, values)
     dv = jnp.dot(probs16, g, preferred_element_type=jnp.float32)
     dk = jnp.dot(dscores, q, preferred_element_type=jnp.float32)
     out_t = jnp.dot(values_t, probs16, preferred_element_type=jnp.float32)
@@ -120,9 +128,12 @@
     return out_t.T.astype(jnp.bfloat16), dq_t.T.astype(jnp.bfloat16), dk, dv
 
 
-def attend_kernel(count, first, last, held, slot_ref, marks_ref, q_ref, g_ref, k_ref, v_ref, *rest):
-    if not first:
-        dk_in, dv_in, *rest = rest
+def numbers(marks):
+    marks = marks.astype(jnp.float32)
+    return marks[:8] * 16.0 + marks[8:]
+
+
+def attend_kernel(count, whole, held, slot_ref, marks_ref, q_ref, g_ref, k_ref, v_ref, *rest):
     o_ref, dq_ref, dk_ref, dv_ref, keys_t, values_t, dk_sum, dv_sum = rest[held:]
     index = pl.program_id(0)
 
@@ -130,11 +141,10 @@
     def _():
         keys_t[...] = k_ref[...].T
         values_t[...] = v_ref[...].T
-        dk_sum[...] = jnp.zeros_like(dk_sum) if first else dk_in[...]
-        dv_sum[...] = jnp.zeros_like(dv_sum) if first else dv_in[...]
-
-    marks = marks_ref[...].astype(jnp.float32)
-    ids = marks[:8] * 16.0 + marks[8:]
+        dk_sum[...] = jnp.zeros_like(dk_sum)
+        dv_sum[...] = jnp.zeros_like(dv_sum)
+
+    ids = numbers(marks_ref[...])
     out, dq, dk, dv = attend_head(
         ids, q_ref[...], g_ref[...], k_ref[...], v_ref[...], keys_t[...], values_t[...]
     )
@@ -145,7 +155,7 @@
 
     @pl.when(index == count - 1)
     def _():
-        if last:
+        if whole:
             dk_ref[...] = (dk_sum[...] * SCALING).astype(jnp.bfloat16)
             dv_ref[...] = dv_sum[...].astype(jnp.bfloat16)
         else:
@@ -153,40 +163,95 @@
             dv_ref[...] = dv_sum[...]
 
 
-def attend(slot, heads, inputs, places, row_count, width, partial=None, held=(), last=True):
+def work(count):
+    return pl.CostEstimate(
+        flops=12 * count * SLOT * SLOT * HEAD_DIM,
+        bytes_accessed=(4 * count + 4) * SLOT * HEAD_DIM * 2,
+        transcendentals=SLOT * SLOT * count,
+    )
+
+
+def attend(slot, heads, inputs, places, row_count, width, held=()):
     def block(place, rows=SLOT):
         return pl.BlockSpec((rows, HEAD_DIM), place)
 
-    first = partial is None
-    wide = block(lambda h, s: (s[0], h + heads[0]))
-    whole = block(lambda h, s: (0, 0))
-    narrow = block(lambda h, s: (s[0], 0)) if last else whole
+    whole = len(held) == 0
+    wide = block(lambda h, s: (s[0], h))
+    narrow = block(lambda h, s: (s[0], 0) if whole else (0, 0))
+    flat = pl.BlockSpec((HEAD_DIM, SLOT), lambda h, s: (0, 0))
     in_specs = [block(places[0], 16)] + [block(place) for place in places[1:]]
-    in_specs += [whole, whole] * (not first) + [pl.BlockSpec(memory_space=pl.ANY)] * len(held)
-    sum_shape = jax.ShapeDtypeStruct((SLOT, HEAD_DIM), jnp.float32)
+    in_specs += [pl.BlockSpec(memory_space=pl.ANY)] * len(held)
     wide_shape = jax.ShapeDtypeStruct((row_count, width), jnp.bfloat16)
     narrow_shape = jax.ShapeDtypeStruct((row_count, HEAD_DIM), jnp.bfloat16)
-    begin = 1 + len(inputs) + 2 * (not first)
+    sum_shape = jax.ShapeDtypeStruct((SLOT, HEAD_DIM), jnp.float32)
+    flat_shape = jax.ShapeDtypeStruct((HEAD_DIM, SLOT), jnp.bfloat16)
     return pl.pallas_call(
-        functools.partial(attend_kernel, len(heads), first, last, len(held)),
-        out_shape=(wide_shape, wide_shape) + ((narrow_shape,) * 2 if last else (sum_shape,) * 2),
+        functools.partial(attend_kernel, len(heads), whole, len(held)),
+        out_shape=(wide_shape,) * 2
+        + ((narrow_shape,) * 2 if whole else (sum_shape,) * 2 + (flat_shape,) * 2),
         grid_spec=pltpu.PrefetchScalarGridSpec(
             num_scalar_prefetch=1,
             grid=(len(heads),),
             in_specs=in_specs,
-            out_specs=(wide, wide, narrow, narrow),
-            scratch_shapes=[pltpu.VMEM((HEAD_DIM, SLOT), jnp.bfloat16)] * 2
+            out_specs=(wide, wide, narrow, narrow) + (flat,) * 2 * (not whole),
+            scratch_shapes=[pltpu.VMEM((HEAD_DIM, SLOT), jnp.bfloat16)] * 2 * whole
             + [pltpu.VMEM((SLOT, HEAD_DIM), jnp.float32)] * 2,
         ),
-        input_output_aliases={begin + i: i for i in range(len(held))},
+        input_output_aliases={1 + len(inputs) + i: i for i in range(len(held))},
         compiler_params=pltpu.CompilerParams(vmem_limit_bytes=16 * 1024 * 1024),
-        cost_estimate=pl.CostEstimate(
-            flops=12 * len(heads) * SLOT * SLOT * HEAD_DIM,
-            bytes_accessed=(4 * len(heads) + 4) * SLOT * HEAD_DIM * 2,
-            transcendentals=SLOT * SLOT * len(heads),
-        ),
+        cost_estimate=work(len(heads)),
         name="attend_" + "_".join(str(h) for h in heads),
-    )(slot, *inputs, *(() if first else partial), *held)
+    )(slot, *inputs, *held)
+
+
+def finish_kernel(head, blocks, slot_ref, most, rest, dk_in, dv_in, keys_t, values_t, *refs):
+    o_ref, dq_ref, dk_ref, dv_ref, made, sems = refs[4:]
+    rows = pl.ds(pl.multiple_of(slot_ref[0] * SLOT, SLOT), SLOT)
+    cols = pl.ds(head * HEAD_DIM, HEAD_DIM)
+    copies = [
+        pltpu.make_async_copy(made.at[i], place, sems.at[i])
+        for i, place in enumerate(
+            (o_ref.at[rows, cols], dq_ref.at[rows, cols], dk_ref.at[rows], dv_ref.at[rows])
+        )
+    ]
+
+    def give(i, value):
+        made[i] = value.astype(jnp.bfloat16)
+        copies[i].start()
+
+    q, g = rest[:SLOT, :], rest[SLOT:, :]
+    keys = most[blocks * SLOT : (blocks + 1) * SLOT, :]
+    values = most[(blocks + 1) * SLOT : (blocks + 2) * SLOT, :]
+    ids = numbers(most[(blocks + 2) * SLOT :, :])
+    probs16, dscores = attend_weights(ids, q, g, keys, values)
+    give(3, dv_in[...] + jnp.dot(probs16, g, preferred_element_type=jnp.float32))
+    give(0, jnp.dot(values_t[...], probs16, preferred_element_type=jnp.float32).T)
+    dk = dk_in[...] + jnp.dot(dscores, q, preferred_element_type=jnp.float32)
+    give(2, dk * SCALING)
+    give(1, (jnp.dot(keys_t[...], dscores, preferred_element_type=jnp.float32) * SCALING).T)
+    for copy in copies:
+        copy.wait()
+
+
+def finish(slot, head, most, rest, sums, held):
+    vmem = pl.BlockSpec(memory_space=pltpu.VMEM)
+    anywhere = pl.BlockSpec(memory_space=pl.ANY)
+    blocks = most.shape[0] // SLOT - 2
+    begin = 3 + len(sums)
+    return pl.pallas_call(
+        functools.partial(finish_kernel, head, blocks),
+        out_shape=tuple(jax.ShapeDtypeStruct(x.shape, x.dtype) for x in held),
+        in_specs=[pl.BlockSpec(memory_space=pltpu.SMEM)] + [vmem] * (begin - 1) + [anywhere] * 4,
+        out_specs=(anywhere,) * 4,
+        scratch_shapes=[
+            pltpu.VMEM((4, SLOT, HEAD_DIM), jnp.bfloat16),
+            pltpu.SemaphoreType.DMA((4,)),
+        ],
+        input_output_aliases={begin + i: i for i in range(4)},
+        compiler_params=pltpu.CompilerParams(vmem_limit_bytes=16 * 1024 * 1024),
+        cost_estimate=work(1),
+        name="finish",
+    )(slot, most, rest, *sums, *held)
 
 
 def body(query_rows, key_rows, value_rows, grad_rows, doc_ids, leaving_group):
@@ -209,7 +274,10 @@
     held = attend(
         staying,
         heads,
-        (marks.reshape(group_count * 16, LANES), query_rows, grad_rows, key_rows, value_rows),
+        (
+            marks.reshape(group_count * 16, LANES),
+            *in_hbm((query_rows, grad_rows, key_rows, value_rows)),
+        ),
         (
             lambda h, s: (s[0], 0),
             lambda h, s: (s[0], h),
@@ -228,7 +296,7 @@
         return (marks_at, 0)
 
     pair_places = (lambda h, s: (pair_at, 0), lambda h, s: (pair_at + 1, 0))
-    out, dq, *partial = attend(
+    out, dq, *sums = attend(
         leaving_group,
         early,
         (most, most, most, most, most),
@@ -241,25 +309,8 @@
         row_count,
         width,
         held=held[:2],
-        last=False,
-    )
-    return tuple(
-        attend(
-            leaving_group,
-            late,
-            (most, rest, rest, most, most),
-            (
-                marks_place,
-                lambda h, s: (0, 0),
-                lambda h, s: (1, 0),
-                *pair_places,
-            ),
-            row_count,
-            width,
-            partial=partial,
-            held=(out, dq, *held[2:]),
-        )
-    )
+    )
+    return tuple(finish(leaving_group, late[0], most, rest, sums, (out, dq, *held[2:])))
 
 
 def solution(mesh):

time: 104 us -> 104 us (level)
  the two profiles are of different devices: /device:TPU:232 before, /device:TPU:236 now
where the time goes in v5:
time: 104 us
  waiting for transfers between devices  72.6 us (70%)
  Pallas kernels  15 us (14%)
  starting transfers between devices  14.6 us (14%)
  between operations  1.35 us (1%)
    ppermute x2, waiting for transfers between devices, swapped(): lax.ppermute(x, axis, [(i, i ^ 1 << bit) for i in range(lax.axis_size(axi...  72.6 us
    ppermute x2, starting transfers between devices, swapped(): lax.ppermute(x, axis, [(i, i ^ 1 << bit) for i in range(lax.axis_size(axi...  14.6 us
    pallas_call x2, Pallas kernels, attend(): pl.pallas_call(functools.partial(attend_kernel, len(heads), whole, len(he...  10.1 us
    pallas_call x2, Pallas kernels, pack(): pl.pallas_call(functools.partial(pack_kernel, heads, whole), out_shape=pa...  3.15 us
  transfers between devices with their start and end apart: 2, of which 2 were waited for; matrix products, arithmetic and copies ran while one was open for 0% of the time, Pallas kernels for 11%

profile of v5, /device:TPU:236, one launch (start us, length us, event | category | flops | bytes accessed | tf_op | source)
XLA Modules:
  0.0 103.5 jit_solution(15296713010008507836)
XLA Ops:
  1.3 2.2 %pack_0_1_2.1 = bf16[3088,128]{1,0:T(8,128)(2,1)S(1)} custom-call(s32[1]{0:T(128)S(6)} %copy.22.slot_ref, bf16[768,512]{1,0:T(8,128)(2,1)} %q_ref, bf16[768,512]{1,0:T(8,128)(2,1)} %g_ref, bf16[768,128]{1,0:T(8,128)(2,1)} %k_ref.1, bf16[768,128]{1,0:T(8,128)(2,1)} %v_ref.1, s32[768]{0:T(1024)} %refs_4_.1), custom_call_target="tpu_custom_call" | custom-call | tf_op jit(solution)/shard_map/pack_0_1_2/pallas_call | solution.py:94
  3.5 0.0 copy-start
  3.5 7.4 %collective-permute-start = (bf16[3088,128]{1,0:T(8,128)(2,1)S(1)}, bf16[3088,128]{1,0:T(8,128)(2,1)S(1)}, u32[]{:S(2)}, u32[]{:S(2)}) collective-permute-start(bf16[3088,128]{1,0:T(8,128)(2,1)S(1)} %pack_0_1_2.1), channel_id=1, source_target_pairs={{0,256},{8,264},{16,272},{24,280},{32,288},{40,296},{48,304},{56,3... | collective-permute-start | bytes 2371592 | tf_op jit(solution)/shard_map/ppermute | solution.py:24
  10.9 1.0 pack_3.1
  11.8 7.2 %collective-permute-start.1 = (bf16[768,128]{1,0:T(8,128)(2,1)S(1)}, bf16[768,128]{1,0:T(8,128)(2,1)S(1)}, u32[]{:S(2)}, u32[]{:S(2)}) collective-permute-start(bf16[768,128]{1,0:T(8,128)(2,1)S(1)} %pack_3.1), channel_id=1, source_target_pairs={{0,256},{8,264},{16,272},{24,280},{32,288},{40,296},{48,304},{56,3... | collective-permute-start | bytes 589832 | tf_op jit(solution)/shard_map/ppermute | solution.py:24
  19.0 0.0 copy-done
  19.1 6.2 %attend_0_1_2_3.1 = (bf16[768,512]{1,0:T(8,128)(2,1)}, bf16[768,512]{1,0:T(8,128)(2,1)}, bf16[768,128]{1,0:T(8,128)(2,1)}, bf16[768,128]{1,0:T(8,128)(2,1)}) custom-call(s32[1]{0:T(128)S(6)} %sub.9.slot_ref, bf16[32,128]{1,0:T(8,128)(2,1)S(1)} %bitcast.1, bf16[768,512]{1,0:T(8,128)(2,1)} %q_ref, bf16[768,512]{1,0:T(8,128)(2,1)} %g_ref, ...), custom_call_target="tpu_custom_call" | custom-call | flops 905969664 | bytes 1966080 | tf_op jit(solution)/shard_map/attend_0_1_2_3/pallas_call | solution.py:188
  25.3 72.3 %collective-permute-done.marks_ref.q_ref.g_ref.k_ref.v_ref.most = bf16[3088,128]{1,0:T(8,128)(2,1)S(1)} collective-permute-done((bf16[3088,128]{1,0:T(8,128)(2,1)S(1)}, bf16[3088,128]{1,0:T(8,128)(2,1)S(1)}, u32[]{:S(2)}, u32[]{:S(2)}) %collective-permute-start) | collective-permute-done | bytes 790560 | tf_op jit(solution)/shard_map/ppermute | solution.py:24
  97.6 3.9 %attend_0_1_2.1 = (bf16[768,512]{1,0:T(8,128)(2,1)}, bf16[768,512]{1,0:T(8,128)(2,1)}, f32[384,128]{1,0:T(8,128)S(1)}, f32[384,128]{1,0:T(8,128)S(1)}, bf16[128,...) custom-call(s32[1]{0:T(128)S(6)} %copy.22.slot_ref, ...), custom_call_target="tpu_custom_call", output_to_operand_aliasing={{0}: (6, {}), {1}: (7, {})} | custom-call | flops 679477248 | bytes 1572864 | tf_op jit(solution)/shard_map/attend_0_1_2/pallas_call | solution.py:188
  101.5 0.3 collective-permute-done.1.rest
  101.8 1.7 %finish.1 = (bf16[768,512]{1,0:T(8,128)(2,1)}, bf16[768,512]{1,0:T(8,128)(2,1)}, bf16[768,128]{1,0:T(8,128)(2,1)}, bf16[768,128]{1,0:T(8,128)(2,1)}) custom-call(s32[1]{0:T(128)S(6)} %copy.22.slot_ref, ...), custom_call_target="tpu_custom_call", output_to_operand_aliasing={{0}: (7, {}), {1}: (8, {}), {2}: (9, {}), {3}: (10, {})} | custom-call | flops 226492416 | bytes 786432 | tf_op jit(solution)/shard_map/finish/pallas_call | solution.py:241
  (3 shorter events, 0.0 us)
Async XLA Ops:
  3.5 15.6 %copy-start = (s32[768]{0:T(1024)S(1)}, s32[768]{0:T(1024)}, u32[]{:S(2)}) copy-start(s32[768]{0:T(1024)} %refs_4_.1) | copy-start | bytes 9220
  3.5 94.1 %collective-permute-start = (bf16[3088,128]{1,0:T(8,128)(2,1)S(1)}, bf16[3088,128]{1,0:T(8,128)(2,1)S(1)}, u32[]{:S(2)}, u32[]{:S(2)}) collective-permute-start(bf16[3088,128]{1,0:T(8,128)(2,1)S(1)} %pack_0_1_2.1), channel_id=1, source_target_pairs={{0,256},{8,264},{16,272},{24,280},{32,288},{40,296},{48,304},{56,3... | collective-permute-start | bytes 2371592 | tf_op jit(solution)/shard_map/ppermute | solution.py:24
  11.8 90.0 %collective-permute-start.1 = (bf16[768,128]{1,0:T(8,128)(2,1)S(1)}, bf16[768,128]{1,0:T(8,128)(2,1)S(1)}, u32[]{:S(2)}, u32[]{:S(2)}) collective-permute-start(bf16[768,128]{1,0:T(8,128)(2,1)S(1)} %pack_3.1), channel_id=1, source_target_pairs={{0,256},{8,264},{16,272},{24,280},{32,288},{40,296},{48,304},{56,3... | collective-permute-start | bytes 589832 | tf_op jit(solution)/shard_map/ppermute | solution.py:24

commit v6 on v5

--- a/solution.py
+++ b/solution.py
@@ -16,7 +16,7 @@
 MASKED = -1e30 * LOG2E
 OVER_LANES = (((1,), (1,)), ((), ()))
 RING = 16
-YIELDING = (5, 7)
+YIELDING = (5, 7, 11, 13)
 HBM = pl.BlockSpec(memory_space=pltpu.HBM)
 
 

time: 104 us -> 103 us (level)
  the two profiles are of different devices: /device:TPU:236 before, /device:TPU:254 now
where the time goes in v6:
time: 103 us
  waiting for transfers between devices  72.2 us (70%)
  Pallas kernels  15 us (15%)
  starting transfers between devices  14.6 us (14%)
  between operations  1.35 us (1%)
    ppermute x2, waiting for transfers between devices, swapped(): lax.ppermute(x, axis, [(i, i ^ 1 << bit) for i in range(lax.axis_size(axi...  72.2 us
    ppermute x2, starting transfers between devices, swapped(): lax.ppermute(x, axis, [(i, i ^ 1 << bit) for i in range(lax.axis_size(axi...  14.6 us
    pallas_call x2, Pallas kernels, attend(): pl.pallas_call(functools.partial(attend_kernel, len(heads), whole, len(he...  10.2 us
    pallas_call x2, Pallas kernels, pack(): pl.pallas_call(functools.partial(pack_kernel, heads, whole), out_shape=pa...  3.15 us
  transfers between devices with their start and end apart: 2, of which 2 were waited for; matrix products, arithmetic and copies ran while one was open for 0% of the time, Pallas kernels for 11%

profile of v6, /device:TPU:254, one launch (start us, length us, event | category | flops | bytes accessed | tf_op | source)
XLA Modules:
  0.0 103.1 jit_solution(9729716417707865854)
XLA Ops:
  1.3 2.2 %pack_0_1_2.1 = bf16[3088,128]{1,0:T(8,128)(2,1)S(1)} custom-call(s32[1]{0:T(128)S(6)} %copy.22.slot_ref, bf16[768,512]{1,0:T(8,128)(2,1)} %q_ref, bf16[768,512]{1,0:T(8,128)(2,1)} %g_ref, bf16[768,128]{1,0:T(8,128)(2,1)} %k_ref.1, bf16[768,128]{1,0:T(8,128)(2,1)} %v_ref.1, s32[768]{0:T(1024)} %refs_4_.1), custom_call_target="tpu_custom_call" | custom-call | tf_op jit(solution)/shard_map/pack_0_1_2/pallas_call | solution.py:94
  3.5 0.0 copy-start
  3.5 7.4 %collective-permute-start = (bf16[3088,128]{1,0:T(8,128)(2,1)S(1)}, bf16[3088,128]{1,0:T(8,128)(2,1)S(1)}, u32[]{:S(2)}, u32[]{:S(2)}) collective-permute-start(bf16[3088,128]{1,0:T(8,128)(2,1)S(1)} %pack_0_1_2.1), channel_id=1, source_target_pairs={{0,256},{8,264},{16,272},{24,280},{32,288},{40,296},{48,304},{56,3... | collective-permute-start | bytes 2371592 | tf_op jit(solution)/shard_map/ppermute | solution.py:24
  10.9 1.0 pack_3.1
  11.8 7.2 %collective-permute-start.1 = (bf16[768,128]{1,0:T(8,128)(2,1)S(1)}, bf16[768,128]{1,0:T(8,128)(2,1)S(1)}, u32[]{:S(2)}, u32[]{:S(2)}) collective-permute-start(bf16[768,128]{1,0:T(8,128)(2,1)S(1)} %pack_3.1), channel_id=1, source_target_pairs={{0,256},{8,264},{16,272},{24,280},{32,288},{40,296},{48,304},{56,3... | collective-permute-start | bytes 589832 | tf_op jit(solution)/shard_map/ppermute | solution.py:24
  19.0 0.0 copy-done
  19.1 6.2 %attend_0_1_2_3.1 = (bf16[768,512]{1,0:T(8,128)(2,1)}, bf16[768,512]{1,0:T(8,128)(2,1)}, bf16[768,128]{1,0:T(8,128)(2,1)}, bf16[768,128]{1,0:T(8,128)(2,1)}) custom-call(s32[1]{0:T(128)S(6)} %sub.9.slot_ref, bf16[32,128]{1,0:T(8,128)(2,1)S(1)} %bitcast.1, bf16[768,512]{1,0:T(8,128)(2,1)} %q_ref, bf16[768,512]{1,0:T(8,128)(2,1)} %g_ref, ...), custom_call_target="tpu_custom_call" | custom-call | flops 905969664 | bytes 1966080 | tf_op jit(solution)/shard_map/attend_0_1_2_3/pallas_call | solution.py:188
  25.3 66.7 %collective-permute-done.marks_ref.q_ref.g_ref.k_ref.v_ref.most = bf16[3088,128]{1,0:T(8,128)(2,1)S(1)} collective-permute-done((bf16[3088,128]{1,0:T(8,128)(2,1)S(1)}, bf16[3088,128]{1,0:T(8,128)(2,1)S(1)}, u32[]{:S(2)}, u32[]{:S(2)}) %collective-permute-start) | collective-permute-done | bytes 790560 | tf_op jit(solution)/shard_map/ppermute | solution.py:24
  92.0 3.9 %attend_0_1_2.1 = (bf16[768,512]{1,0:T(8,128)(2,1)}, bf16[768,512]{1,0:T(8,128)(2,1)}, f32[384,128]{1,0:T(8,128)S(1)}, f32[384,128]{1,0:T(8,128)S(1)}, bf16[128,...) custom-call(s32[1]{0:T(128)S(6)} %copy.22.slot_ref, ...), custom_call_target="tpu_custom_call", output_to_operand_aliasing={{0}: (6, {}), {1}: (7, {})} | custom-call | flops 679477248 | bytes 1572864 | tf_op jit(solution)/shard_map/attend_0_1_2/pallas_call | solution.py:188
  95.9 5.5 %collective-permute-done.1.rest = bf16[768,128]{1,0:T(8,128)(2,1)S(1)} collective-permute-done((bf16[768,128]{1,0:T(8,128)(2,1)S(1)}, bf16[768,128]{1,0:T(8,128)(2,1)S(1)}, u32[]{:S(2)}, u32[]{:S(2)}) %collective-permute-start.1) | collective-permute-done | bytes 196640 | tf_op jit(solution)/shard_map/ppermute | solution.py:24
  101.5 1.7 %finish.1 = (bf16[768,512]{1,0:T(8,128)(2,1)}, bf16[768,512]{1,0:T(8,128)(2,1)}, bf16[768,128]{1,0:T(8,128)(2,1)}, bf16[768,128]{1,0:T(8,128)(2,1)}) custom-call(s32[1]{0:T(128)S(6)} %copy.22.slot_ref, ...), custom_call_target="tpu_custom_call", output_to_operand_aliasing={{0}: (7, {}), {1}: (8, {}), {2}: (9, {}), {3}: (10, {})} | custom-call | flops 226492416 | bytes 786432 | tf_op jit(solution)/shard_map/finish/pallas_call | solution.py:241
  (3 shorter events, 0.0 us)
Async XLA Ops:
  3.5 15.6 %copy-start = (s32[768]{0:T(1024)S(1)}, s32[768]{0:T(1024)}, u32[]{:S(2)}) copy-start(s32[768]{0:T(1024)} %refs_4_.1) | copy-start | bytes 9220
  3.5 88.6 %collective-permute-start = (bf16[3088,128]{1,0:T(8,128)(2,1)S(1)}, bf16[3088,128]{1,0:T(8,128)(2,1)S(1)}, u32[]{:S(2)}, u32[]{:S(2)}) collective-permute-start(bf16[3088,128]{1,0:T(8,128)(2,1)S(1)} %pack_0_1_2.1), channel_id=1, source_target_pairs={{0,256},{8,264},{16,272},{24,280},{32,288},{40,296},{48,304},{56,3... | collective-permute-start | bytes 2371592 | tf_op jit(solution)/shard_map/ppermute | solution.py:24
  11.8 89.6 %collective-permute-start.1 = (bf16[768,128]{1,0:T(8,128)(2,1)S(1)}, bf16[768,128]{1,0:T(8,128)(2,1)S(1)}, u32[]{:S(2)}, u32[]{:S(2)}) collective-permute-start(bf16[768,128]{1,0:T(8,128)(2,1)S(1)} %pack_3.1), channel_id=1, source_target_pairs={{0,256},{8,264},{16,272},{24,280},{32,288},{40,296},{48,304},{56,3... | collective-permute-start | bytes 589832 | tf_op jit(solution)/shard_map/ppermute | solution.py:24

commit v7 on v6

--- a/solution.py
+++ b/solution.py
@@ -28,7 +28,7 @@
     return [pltpu.with_memory_space_constraint(x, pltpu.HBM) for x in arrays]
 
 
-def pack_kernel(heads, whole, slot_ref, *refs):
+def pack_kernel(q_heads, g_heads, whole, slot_ref, *refs):
     if whole:
         *inputs, ids_ref, out_ref, ids, sems = refs
         ids_copy = pltpu.make_async_copy(ids_ref, ids, sems.at[sems.shape[0] - 1])
@@ -37,7 +37,9 @@
         *inputs, out_ref, sems = refs
     rows = pl.ds(pl.multiple_of(slot_ref[0] * SLOT, SLOT), SLOT)
     parts = [
-        ref.at[rows, pl.ds(h * HEAD_DIM, HEAD_DIM)] for ref in inputs[:2] for h in heads
+        ref.at[rows, pl.ds(h * HEAD_DIM, HEAD_DIM)]
+        for ref, heads in zip(inputs, (q_heads, g_heads))
+        for h in heads
     ]
     parts += [ref.at[rows] for ref in inputs[2:]]
     copies = [
@@ -84,27 +86,26 @@
             copy.wait()
 
 
-def pack(slot, heads, query, grad, pair=(), doc_ids=None):
+def pack(slot, q_heads, g_heads, query, grad, pair=(), doc_ids=None):
     whole = doc_ids is not None
-    count = 2 * len(heads) + len(pair)
+    count = len(q_heads) + len(g_heads) + len(pair)
     inputs = (query, grad, *pair) + ((doc_ids,) if whole else ())
     inputs = in_hbm(inputs)
     packed = jax.ShapeDtypeStruct((count * SLOT + 16 * whole, HEAD_DIM), query.dtype)
     scratch = [pltpu.VMEM(doc_ids.shape, jnp.int32)] if whole else []
     return pl.pallas_call(
-        functools.partial(pack_kernel, heads, whole),
+        functools.partial(pack_kernel, q_heads, g_heads, whole),
         out_shape=packed,
         in_specs=[pl.BlockSpec(memory_space=pltpu.SMEM)] + [HBM] * len(inputs),
         out_specs=pl.BlockSpec(memory_space=pltpu.VMEM),
         scratch_shapes=scratch + [pltpu.SemaphoreType.DMA((count + whole,))],
         compiler_params=pltpu.CompilerParams(vmem_limit_bytes=4 * 1024 * 1024),
-        name="pack_" + "_".join(str(h) for h in heads),
+        name=f"pack_{count}",
     )(slot, *inputs)
 
 
-def attend_weights(ids, q, g, keys, values):
+def attend_probs(ids, q, keys):
     scores = lax.dot_general(keys, q, OVER_LANES, preferred_element_type=jnp.float32)
-    dprobs = lax.dot_general(values, g, OVER_LANES, preferred_element_type=jnp.float32)
     ids_t = ids.T
     key_ids = jnp.concatenate([ids_t[:, j : j + 1] for j in range(RUNS)], axis=0)
     row_ids = jnp.concatenate([ids[j : j + 1, :] for j in range(RUNS)], axis=1)
@@ -113,14 +114,19 @@
     allowed = (key_ids == row_ids) & (key_places <= row_places)
     scores = jnp.where(allowed, scores * (SCALING * LOG2E), MASKED)
     weights = jnp.exp2(scores - jnp.max(scores, axis=0, keepdims=True))
-    probs = weights * (1.0 / jnp.sum(weights, axis=0, keepdims=True))
+    return weights * (1.0 / jnp.sum(weights, axis=0, keepdims=True))
+
+
+def attend_dscores(probs, g, values):
+    dprobs = lax.dot_general(values, g, OVER_LANES, preferred_element_type=jnp.float32)
     inner_sum = jnp.sum(probs * dprobs, axis=0, keepdims=True)
+    return (probs * (dprobs - inner_sum)).astype(jnp.bfloat16)
+
+
+def attend_head(ids, q, g, keys, values, keys_t, values_t):
+    probs = attend_probs(ids, q, keys)
     probs16 = probs.astype(jnp.bfloat16)
-    return probs16, (probs * (dprobs - inner_sum)).astype(jnp.bfloat16)
-
-
-def attend_head(ids, q, g, keys, values, keys_t, values_t):
-    probs16, dscores = attend_weights(ids, q, g, keys, values)
+    dscores = attend_dscores(probs, g, values)
     dv = jnp.dot(probs16, g, preferred_element_type=jnp.float32)
     dk = jnp.dot(dscores, q, preferred_element_type=jnp.float32)
     out_t = jnp.dot(values_t, probs16, preferred_element_type=jnp.float32)
@@ -204,68 +210,111 @@
     )(slot, *inputs, *held)
 
 
-def finish_kernel(head, blocks, slot_ref, most, rest, dk_in, dv_in, keys_t, values_t, *refs):
-    o_ref, dq_ref, dk_ref, dv_ref, made, sems = refs[4:]
-    rows = pl.ds(pl.multiple_of(slot_ref[0] * SLOT, SLOT), SLOT)
-    cols = pl.ds(head * HEAD_DIM, HEAD_DIM)
+def product(a, b):
+    return jnp.dot(a, b, preferred_element_type=jnp.float32)
+
+
+def giver(made, places, sems):
     copies = [
-        pltpu.make_async_copy(made.at[i], place, sems.at[i])
-        for i, place in enumerate(
-            (o_ref.at[rows, cols], dq_ref.at[rows, cols], dk_ref.at[rows], dv_ref.at[rows])
-        )
+        pltpu.make_async_copy(made.at[i], place, sems.at[i]) for i, place in enumerate(places)
     ]
 
     def give(i, value):
         made[i] = value.astype(jnp.bfloat16)
         copies[i].start()
 
-    q, g = rest[:SLOT, :], rest[SLOT:, :]
-    keys = most[blocks * SLOT : (blocks + 1) * SLOT, :]
-    values = most[(blocks + 1) * SLOT : (blocks + 2) * SLOT, :]
+    def settle():
+        for copy in copies:
+            copy.wait()
+
+    return give, settle
+
+
+def lanes(head):
+    return pl.ds(head * HEAD_DIM, HEAD_DIM)
+
+
+def part(ref, i):
+    return ref[i * SLOT : (i + 1) * SLOT, :]
+
+
+def middle_kernel(heads, blocks, slot_ref, most, mid, dk_in, dv_in, keys_t, values_t, *refs):
+    o_ref, dq_ref, dk_ref, dv_ref, probs_ref, probs16_ref, made, sems = refs[2:]
+    rows = pl.ds(pl.multiple_of(slot_ref[0] * SLOT, SLOT), SLOT)
+    full, begun = heads
+    places = (o_ref.at[rows, lanes(full)], dq_ref.at[rows, lanes(full)], o_ref.at[rows, lanes(begun)])
+    give, settle = giver(made, places, sems)
+    keys, values = part(most, blocks), part(most, blocks + 1)
     ids = numbers(most[(blocks + 2) * SLOT :, :])
-    probs16, dscores = attend_weights(ids, q, g, keys, values)
-    give(3, dv_in[...] + jnp.dot(probs16, g, preferred_element_type=jnp.float32))
-    give(0, jnp.dot(values_t[...], probs16, preferred_element_type=jnp.float32).T)
-    dk = dk_in[...] + jnp.dot(dscores, q, preferred_element_type=jnp.float32)
-    give(2, dk * SCALING)
-    give(1, (jnp.dot(keys_t[...], dscores, preferred_element_type=jnp.float32) * SCALING).T)
-    for copy in copies:
-        copy.wait()
-
-
-def finish(slot, head, most, rest, sums, held):
+    q, g = part(mid, 0), part(mid, 2)
+    probs = attend_probs(ids, q, keys)
+    probs16 = probs.astype(jnp.bfloat16)
+    dscores = attend_dscores(probs, g, values)
+    give(0, product(values_t[...], probs16).T)
+    give(1, (product(keys_t[...], dscores) * SCALING).T)
+    dv_ref[...] = dv_in[...] + product(probs16, g)
+    dk_ref[...] = dk_in[...] + product(dscores, q)
+    probs = attend_probs(ids, part(mid, 1), keys)
+    probs16 = probs.astype(jnp.bfloat16)
+    probs_ref[...] = probs
+    probs16_ref[...] = probs16
+    give(2, product(values_t[...], probs16).T)
+    settle()
+
+
+def finish_kernel(
+    head, blocks, slot_ref, most, mid, last, dk_in, dv_in, probs_ref, probs16_ref, keys_t, *refs
+):
+    dq_ref, dk_ref, dv_ref, made, sems = refs[3:]
+    rows = pl.ds(pl.multiple_of(slot_ref[0] * SLOT, SLOT), SLOT)
+    places = (dq_ref.at[rows, lanes(head)], dk_ref.at[rows], dv_ref.at[rows])
+    give, settle = giver(made, places, sems)
+    q, g = part(mid, 1), last[...]
+    dscores = attend_dscores(probs_ref[...], g, part(most, blocks + 1))
+    give(2, dv_in[...] + product(probs16_ref[...], g))
+    give(1, (dk_in[...] + product(dscores, q)) * SCALING)
+    give(0, (product(keys_t[...], dscores) * SCALING).T)
+    settle()
+
+
+def one_step(kernel, name, slot, inputs, held, shapes, cost):
     vmem = pl.BlockSpec(memory_space=pltpu.VMEM)
     anywhere = pl.BlockSpec(memory_space=pl.ANY)
-    blocks = most.shape[0] // SLOT - 2
-    begin = 3 + len(sums)
     return pl.pallas_call(
-        functools.partial(finish_kernel, head, blocks),
-        out_shape=tuple(jax.ShapeDtypeStruct(x.shape, x.dtype) for x in held),
-        in_specs=[pl.BlockSpec(memory_space=pltpu.SMEM)] + [vmem] * (begin - 1) + [anywhere] * 4,
-        out_specs=(anywhere,) * 4,
+        kernel,
+        out_shape=tuple(jax.ShapeDtypeStruct(x.shape, x.dtype) for x in held) + shapes,
+        in_specs=[pl.BlockSpec(memory_space=pltpu.SMEM)]
+        + [vmem] * len(inputs)
+        + [anywhere] * len(held),
+        out_specs=(anywhere,) * len(held) + (vmem,) * len(shapes),
         scratch_shapes=[
-            pltpu.VMEM((4, SLOT, HEAD_DIM), jnp.bfloat16),
-            pltpu.SemaphoreType.DMA((4,)),
+            pltpu.VMEM((3, SLOT, HEAD_DIM), jnp.bfloat16),
+            pltpu.SemaphoreType.DMA((3,)),
         ],
-        input_output_aliases={begin + i: i for i in range(4)},
+        input_output_aliases={1 + len(inputs) + i: i for i in range(len(held))},
         compiler_params=pltpu.CompilerParams(vmem_limit_bytes=16 * 1024 * 1024),
-        cost_estimate=work(1),
-        name="finish",
-    )(slot, most, rest, *sums, *held)
+        cost_estimate=work(cost),
+        name=name,
+    )(slot, *inputs, *held)
 
 
 def body(query_rows, key_rows, value_rows, grad_rows, doc_ids, leaving_group):
     row_count, width = query_rows.shape
     heads = tuple(range(width // HEAD_DIM))
-    early, late = heads[:-1], heads[-1:]
+    early, late = heads[:-2], heads[-2:]
     group_count = row_count // SLOT
     far_bit = lax.axis_size("dp").bit_length() - 2
 
-    most = pack(leaving_group, early, query_rows, grad_rows, (key_rows, value_rows), doc_ids)
+    most = pack(
+        leaving_group, early, early, query_rows, grad_rows, (key_rows, value_rows), doc_ids
+    )
     most, query_rows, grad_rows = lax.optimization_barrier((most, query_rows, grad_rows))
     most = swapped(most, "dp", far_bit)
-    rest = pack(leaving_group, late, query_rows, grad_rows)
-    rest = swapped(rest, "dp", far_bit)
+    mid = pack(leaving_group, late, late[:1], query_rows, grad_rows)
+    mid, query_rows, grad_rows = lax.optimization_barrier((mid, query_rows, grad_rows))
+    mid = swapped(mid, "dp", far_bit)
+    last = pack(leaving_group, (), late[1:], query_rows, grad_rows)
+    last = swapped(last, "dp", far_bit)
 
     ids = jnp.pad(doc_ids.reshape(group_count, RUNS, LANES), ((0, 0), (0, 8 - RUNS), (0, 0)))
     marks = jnp.concatenate([ids // 16, ids % 16], axis=1).astype(jnp.bfloat16)
@@ -296,7 +345,7 @@
         return (marks_at, 0)
 
     pair_places = (lambda h, s: (pair_at, 0), lambda h, s: (pair_at + 1, 0))
-    out, dq, *sums = attend(
+    out, dq, dk_sum, dv_sum, keys_t, values_t = attend(
         leaving_group,
         early,
         (most, most, most, most, most),
@@ -310,7 +359,27 @@
         width,
         held=held[:2],
     )
-    return tuple(finish(leaving_group, late[0], most, rest, sums, (out, dq, *held[2:])))
+    sum_shape = jax.ShapeDtypeStruct((SLOT, HEAD_DIM), jnp.float32)
+    square = [jax.ShapeDtypeStruct((SLOT, SLOT), t) for t in (jnp.float32, jnp.bfloat16)]
+    out, dq, *sums = one_step(
+        functools.partial(middle_kernel, late, pair_at),
+        "middle",
+        leaving_group,
+        (most, mid, dk_sum, dv_sum, keys_t, values_t),
+        (out, dq),
+        (sum_shape, sum_shape, *square),
+        2,
+    )
+    dq, dk, dv = one_step(
+        functools.partial(finish_kernel, late[1], pair_at),
+        "finish",
+        leaving_group,
+        (most, mid, last, *sums, keys_t),
+        (dq, *held[2:]),
+        (),
+        1,
+    )
+    return out, dq, dk, dv
 
 
 def solution(mesh):

time: 103 us -> 104 us (level)
  the two profiles are of different devices: /device:TPU:254 before, /device:TPU:252 now
where the time goes in v7:
time: 104 us
  waiting for transfers between devices  63.9 us (61%)
  starting transfers between devices  21.9 us (21%)
  Pallas kernels  16.6 us (16%)
  between operations  1.38 us (1%)
    ppermute x3, waiting for transfers between devices, swapped(): lax.ppermute(x, axis, [(i, i ^ 1 << bit) for i in range(lax.axis_size(axi...  63.9 us
    ppermute x3, starting transfers between devices, swapped(): lax.ppermute(x, axis, [(i, i ^ 1 << bit) for i in range(lax.axis_size(axi...  21.9 us
    pallas_call x2, Pallas kernels, attend(): pl.pallas_call(functools.partial(attend_kernel, len(heads), whole, len(he...  9.09 us
    pallas_call x3, Pallas kernels, pack(): pl.pallas_call(functools.partial(pack_kernel, q_heads, g_heads, whole), o...  4 us
    pallas_call x2, Pallas kernels, one_step(): pl.pallas_call(kernel, out_shape=tuple((jax.ShapeDtypeStruct(x.shape, x.d...  3.48 us
  transfers between devices with their start and end apart: 3, of which 2 were waited for; matrix products, arithmetic and copies ran while one was open for 0% of the time, Pallas kernels for 13%

profile of v7, /device:TPU:252, one launch (start us, length us, event | category | flops | bytes accessed | tf_op | source)
XLA Modules:
  0.0 103.8 jit_solution(9805952883887884269)
XLA Ops:
  1.3 2.1 %pack_6.1 = bf16[2320,128]{1,0:T(8,128)(2,1)S(1)} custom-call(s32[1]{0:T(128)S(6)} %copy.24.slot_ref, bf16[768,512]{1,0:T(8,128)(2,1)} %refs_0_.3, bf16[768,512]{1,0:T(8,128)(2,1)} %refs_1_.3, bf16[768,128]{1,0:T(8,128)(2,1)} %k_ref.1, bf16[768,128]{1,0:T(8,128)(2,1)} %v_ref.1, s32[768]{0:T(1024)} %refs_4_.1), custom_call_target="tpu_custom_call" | custom-call | tf_op jit(solution)/shard_map/pack_6/pallas_call | solution.py:96
  3.3 7.4 %collective-permute-start = (bf16[2320,128]{1,0:T(8,128)(2,1)S(1)}, bf16[2320,128]{1,0:T(8,128)(2,1)S(1)}, u32[]{:S(2)}, u32[]{:S(2)}) collective-permute-start(bf16[2320,128]{1,0:T(8,128)(2,1)S(1)} %pack_6.1), channel_id=1, source_target_pairs={{0,256},{8,264},{16,272},{24,280},{32,288},{40,296},{48,304},{56,3... | collective-permute-start | bytes 1781768 | tf_op jit(solution)/shard_map/ppermute | solution.py:24
  10.7 1.0 pack_3.1
  11.8 0.0 copy-start
  11.8 7.2 %collective-permute-start.1 = (bf16[1152,128]{1,0:T(8,128)(2,1)S(1)}, bf16[1152,128]{1,0:T(8,128)(2,1)S(1)}, u32[]{:S(2)}, u32[]{:S(2)}) collective-permute-start(bf16[1152,128]{1,0:T(8,128)(2,1)S(1)} %pack_3.1), channel_id=1, source_target_pairs={{0,256},{8,264},{16,272},{24,280},{32,288},{40,296},{48,304},{56,3... | collective-permute-start | bytes 884744 | tf_op jit(solution)/shard_map/ppermute | solution.py:24
  19.0 0.9 pack_1.1
  19.9 7.4 %collective-permute-start.2 = (bf16[384,128]{1,0:T(8,128)(2,1)S(1)}, bf16[384,128]{1,0:T(8,128)(2,1)S(1)}, u32[]{:S(2)}, u32[]{:S(2)}) collective-permute-start(bf16[384,128]{1,0:T(8,128)(2,1)S(1)} %pack_1.1), channel_id=1, source_target_pairs={{0,256},{8,264},{16,272},{24,280},{32,288},{40,296},{48,304},{56,3... | collective-permute-start | bytes 294920 | tf_op jit(solution)/shard_map/ppermute | solution.py:24
  27.3 0.0 copy-done
  27.3 6.2 %attend_0_1_2_3.1 = (bf16[768,512]{1,0:T(8,128)(2,1)}, bf16[768,512]{1,0:T(8,128)(2,1)}, bf16[768,128]{1,0:T(8,128)(2,1)}, bf16[768,128]{1,0:T(8,128)(2,1)}) custom-call(s32[1]{0:T(128)S(6)} %sub.9.slot_ref, bf16[32,128]{1,0:T(8,128)(2,1)S(1)} %bitcast.1, bf16[768,512]{1,0:T(8,128)(2,1)} %refs_0_.3, bf16[768,512]{1,0:T(8,128)(2,1)} %refs_1_.3, ...), custom_call_target="tpu_custom_call" | custom-call | flops 905969664 | bytes 1966080 | tf_op jit(solution)/shard_map/attend_0_1_2_3/pallas_call | solution.py:194
  33.6 38.8 %collective-permute-done.marks_ref.q_ref.g_ref.k_ref.v_ref.most = bf16[2320,128]{1,0:T(8,128)(2,1)S(1)} collective-permute-done((bf16[2320,128]{1,0:T(8,128)(2,1)S(1)}, bf16[2320,128]{1,0:T(8,128)(2,1)S(1)}, u32[]{:S(2)}, u32[]{:S(2)}) %collective-permute-start) | collective-permute-done | bytes 593952 | tf_op jit(solution)/shard_map/ppermute | solution.py:24
  72.4 2.9 %attend_0_1.1 = (bf16[768,512]{1,0:T(8,128)(2,1)}, bf16[768,512]{1,0:T(8,128)(2,1)}, f32[384,128]{1,0:T(8,128)S(1)}, f32[384,128]{1,0:T(8,128)S(1)}, bf16[128,38...) custom-call(s32[1]{0:T(128)S(6)} %copy.24.slot_ref, ...), custom_call_target="tpu_custom_call", output_to_operand_aliasing={{0}: (6, {}), {1}: (7, {})} | custom-call | flops 452984832 | bytes 1179648 | tf_op jit(solution)/shard_map/attend_0_1/pallas_call | solution.py:194
  75.3 25.0 %collective-permute-done.1.mid = bf16[1152,128]{1,0:T(8,128)(2,1)S(1)} collective-permute-done((bf16[1152,128]{1,0:T(8,128)(2,1)S(1)}, bf16[1152,128]{1,0:T(8,128)(2,1)S(1)}, u32[]{:S(2)}, u32[]{:S(2)}) %collective-permute-start.1) | collective-permute-done | bytes 294944 | tf_op jit(solution)/shard_map/ppermute | solution.py:24
  100.3 2.1 %middle.1 = (bf16[768,512]{1,0:T(8,128)(2,1)}, bf16[768,512]{1,0:T(8,128)(2,1)}, f32[384,128]{1,0:T(8,128)S(1)}, f32[384,128]{1,0:T(8,128)S(1)}, f32[384,384]{1,0:T(8,128)S(1)}, /*index=5*/bf16[384,384]{1,0:T(8,128)(2,1)S(1)}) custom-call(s32[1]{0:T(128)S(6)} %copy.24.slot_ref, ...), custom_call_target="tpu_custom_call", output_to_operand_aliasing={{0}: (7, {}), {1}: (8, {})} | custom-call | flops 452984832 | bytes 1179648 | tf_op jit(solution)/shard_map/middle/pallas_call | solution.py:283
  102.4 0.0 collective-permute-done.2.last
  102.4 1.4 %finish.1 = (bf16[768,512]{1,0:T(8,128)(2,1)}, bf16[768,128]{1,0:T(8,128)(2,1)}, bf16[768,128]{1,0:T(8,128)(2,1)}) custom-call(s32[1]{0:T(128)S(6)} %copy.24.slot_ref, bf16[2320,128]{1,0:T(8,128)(2,1)S(1)} %collective-permute-done.marks_ref.q_ref.g_ref.k_ref.v_ref.most, ...), custom_call_target="tpu_custom_call", output_to_operand_aliasing={{0}: (9, {}), {1}: (10, {}), {2}: (11, {})} | custom-call | flops 226492416 | bytes 786432 | tf_op jit(solution)/shard_map/finish/pallas_call | solution.py:283
  (3 shorter events, 0.0 us)
Async XLA Ops:
  3.3 69.0 %collective-permute-start = (bf16[2320,128]{1,0:T(8,128)(2,1)S(1)}, bf16[2320,128]{1,0:T(8,128)(2,1)S(1)}, u32[]{:S(2)}, u32[]{:S(2)}) collective-permute-start(bf16[2320,128]{1,0:T(8,128)(2,1)S(1)} %pack_6.1), channel_id=1, source_target_pairs={{0,256},{8,264},{16,272},{24,280},{32,288},{40,296},{48,304},{56,3... | collective-permute-start | bytes 1781768 | tf_op jit(solution)/shard_map/ppermute | solution.py:24
  11.8 15.5 %copy-start = (s32[768]{0:T(1024)S(1)}, s32[768]{0:T(1024)}, u32[]{:S(2)}) copy-start(s32[768]{0:T(1024)} %refs_4_.1) | copy-start | bytes 9220
  11.8 88.5 %collective-permute-start.1 = (bf16[1152,128]{1,0:T(8,128)(2,1)S(1)}, bf16[1152,128]{1,0:T(8,128)(2,1)S(1)}, u32[]{:S(2)}, u32[]{:S(2)}) collective-permute-start(bf16[1152,128]{1,0:T(8,128)(2,1)S(1)} %pack_3.1), channel_id=1, source_target_pairs={{0,256},{8,264},{16,272},{24,280},{32,288},{40,296},{48,304},{56,3... | collective-permute-start | bytes 884744 | tf_op jit(solution)/shard_map/ppermute | solution.py:24
  19.9 82.5 %collective-permute-start.2 = (bf16[384,128]{1,0:T(8,128)(2,1)S(1)}, bf16[384,128]{1,0:T(8,128)(2,1)S(1)}, u32[]{:S(2)}, u32[]{:S(2)}) collective-permute-start(bf16[384,128]{1,0:T(8,128)(2,1)S(1)} %pack_1.1), channel_id=1, source_target_pairs={{0,256},{8,264},{16,272},{24,280},{32,288},{40,296},{48,304},{56,3... | collective-permute-start | bytes 294920 | tf_op jit(solution)/shard_map/ppermute | solution.py:24

commit v8 on v7

--- a/solution.py
+++ b/solution.py
@@ -139,8 +139,8 @@
     return marks[:8] * 16.0 + marks[8:]
 
 
-def attend_kernel(count, whole, held, slot_ref, marks_ref, q_ref, g_ref, k_ref, v_ref, *rest):
-    o_ref, dq_ref, dk_ref, dv_ref, keys_t, values_t, dk_sum, dv_sum = rest[held:]
+def attend_kernel(count, slot_ref, marks_ref, q_ref, g_ref, k_ref, v_ref, *rest):
+    o_ref, dq_ref, dk_ref, dv_ref, keys_t, values_t, dk_sum, dv_sum = rest
     index = pl.program_id(0)
 
     @pl.when(index == 0)
@@ -161,12 +161,8 @@
 
     @pl.when(index == count - 1)
     def _():
-        if whole:
-            dk_ref[...] = (dk_sum[...] * SCALING).astype(jnp.bfloat16)
-            dv_ref[...] = dv_sum[...].astype(jnp.bfloat16)
-        else:
-            dk_ref[...] = dk_sum[...]
-            dv_ref[...] = dv_sum[...]
+        dk_ref[...] = (dk_sum[...] * SCALING).astype(jnp.bfloat16)
+        dv_ref[...] = dv_sum[...].astype(jnp.bfloat16)
 
 
 def work(count):
@@ -177,37 +173,29 @@
     )
 
 
-def attend(slot, heads, inputs, places, row_count, width, held=()):
+def attend(slot, heads, inputs, places, row_count, width):
     def block(place, rows=SLOT):
         return pl.BlockSpec((rows, HEAD_DIM), place)
 
-    whole = len(held) == 0
     wide = block(lambda h, s: (s[0], h))
-    narrow = block(lambda h, s: (s[0], 0) if whole else (0, 0))
-    flat = pl.BlockSpec((HEAD_DIM, SLOT), lambda h, s: (0, 0))
-    in_specs = [block(places[0], 16)] + [block(place) for place in places[1:]]
-    in_specs += [pl.BlockSpec(memory_space=pl.ANY)] * len(held)
+    narrow = block(lambda h, s: (s[0], 0))
     wide_shape = jax.ShapeDtypeStruct((row_count, width), jnp.bfloat16)
     narrow_shape = jax.ShapeDtypeStruct((row_count, HEAD_DIM), jnp.bfloat16)
-    sum_shape = jax.ShapeDtypeStruct((SLOT, HEAD_DIM), jnp.float32)
-    flat_shape = jax.ShapeDtypeStruct((HEAD_DIM, SLOT), jnp.bfloat16)
     return pl.pallas_call(
-        functools.partial(attend_kernel, len(heads), whole, len(held)),
-        out_shape=(wide_shape,) * 2
-        + ((narrow_shape,) * 2 if whole else (sum_shape,) * 2 + (flat_shape,) * 2),
+        functools.partial(attend_kernel, len(heads)),
+        out_shape=(wide_shape,) * 2 + (narrow_shape,) * 2,
         grid_spec=pltpu.PrefetchScalarGridSpec(
             num_scalar_prefetch=1,
             grid=(len(heads),),
-            in_specs=in_specs,
-            out_specs=(wide, wide, narrow, narrow) + (flat,) * 2 * (not whole),
-            scratch_shapes=[pltpu.VMEM((HEAD_DIM, SLOT), jnp.bfloat16)] * 2 * whole
+            in_specs=[block(places[0], 16)] + [block(place) for place in places[1:]],
+            out_specs=(wide, wide, narrow, narrow),
+            scratch_shapes=[pltpu.VMEM((HEAD_DIM, SLOT), jnp.bfloat16)] * 2
             + [pltpu.VMEM((SLOT, HEAD_DIM), jnp.float32)] * 2,
         ),
-        input_output_aliases={1 + len(inputs) + i: i for i in range(len(held))},
         compiler_params=pltpu.CompilerParams(vmem_limit_bytes=16 * 1024 * 1024),
         cost_estimate=work(len(heads)),
-        name="attend_" + "_".join(str(h) for h in heads),
-    )(slot, *inputs, *held)
+        name="attend_staying",
+    )(slot, *inputs)
 
 
 def product(a, b):
@@ -238,46 +226,46 @@
     return ref[i * SLOT : (i + 1) * SLOT, :]
 
 
-def middle_kernel(heads, blocks, slot_ref, most, mid, dk_in, dv_in, keys_t, values_t, *refs):
-    o_ref, dq_ref, dk_ref, dv_ref, probs_ref, probs16_ref, made, sems = refs[2:]
+def early_kernel(heads, blocks, slot_ref, most, *refs):
+    o_ref, dq_ref, dk_ref, dv_ref, keys_t, values_t, made, sems = refs[2:]
     rows = pl.ds(pl.multiple_of(slot_ref[0] * SLOT, SLOT), SLOT)
-    full, begun = heads
-    places = (o_ref.at[rows, lanes(full)], dq_ref.at[rows, lanes(full)], o_ref.at[rows, lanes(begun)])
+    places = [ref.at[rows, lanes(h)] for h in heads for ref in (o_ref, dq_ref)]
     give, settle = giver(made, places, sems)
     keys, values = part(most, blocks), part(most, blocks + 1)
     ids = numbers(most[(blocks + 2) * SLOT :, :])
-    q, g = part(mid, 0), part(mid, 2)
-    probs = attend_probs(ids, q, keys)
+    keys_t[...] = keys.T
+    values_t[...] = values.T
+    for i in range(len(heads)):
+        q, g = part(most, i), part(most, len(heads) + i)
+        probs = attend_probs(ids, q, keys)
+        probs16 = probs.astype(jnp.bfloat16)
+        dscores = attend_dscores(probs, g, values)
+        give(2 * i, product(values_t[...], probs16).T)
+        give(2 * i + 1, (product(keys_t[...], dscores) * SCALING).T)
+        dv, dk = product(probs16, g), product(dscores, q)
+        dv_ref[...] = dv if i == 0 else dv_ref[...] + dv
+        dk_ref[...] = dk if i == 0 else dk_ref[...] + dk
+    settle()
+
+
+def finish_kernel(head, blocks, slot_ref, most, rest, dk_in, dv_in, keys_t, values_t, *refs):
+    o_ref, dq_ref, dk_ref, dv_ref, made, sems = refs[4:]
+    rows = pl.ds(pl.multiple_of(slot_ref[0] * SLOT, SLOT), SLOT)
+    places = (o_ref.at[rows, lanes(head)], dq_ref.at[rows, lanes(head)])
+    give, settle = giver(made, places + (dk_ref.at[rows], dv_ref.at[rows]), sems)
+    ids = numbers(most[(blocks + 2) * SLOT :, :])
+    q, g = part(rest, 0), part(rest, 1)
+    probs = attend_probs(ids, q, part(most, blocks))
     probs16 = probs.astype(jnp.bfloat16)
-    dscores = attend_dscores(probs, g, values)
+    dscores = attend_dscores(probs, g, part(most, blocks + 1))
+    give(3, dv_in[...] + product(probs16, g))
     give(0, product(values_t[...], probs16).T)
+    give(2, (dk_in[...] + product(dscores, q)) * SCALING)
     give(1, (product(keys_t[...], dscores) * SCALING).T)
-    dv_ref[...] = dv_in[...] + product(probs16, g)
-    dk_ref[...] = dk_in[...] + product(dscores, q)
-    probs = attend_probs(ids, part(mid, 1), keys)
-    probs16 = probs.astype(jnp.bfloat16)
-    probs_ref[...] = probs
-    probs16_ref[...] = probs16
-    give(2, product(values_t[...], probs16).T)
     settle()
 
 
-def finish_kernel(
-    head, blocks, slot_ref, most, mid, last, dk_in, dv_in, probs_ref, probs16_ref, keys_t, *refs
-):
-    dq_ref, dk_ref, dv_ref, made, sems = refs[3:]
-    rows = pl.ds(pl.multiple_of(slot_ref[0] * SLOT, SLOT), SLOT)
-    places = (dq_ref.at[rows, lanes(head)], dk_ref.at[rows], dv_ref.at[rows])
-    give, settle = giver(made, places, sems)
-    q, g = part(mid, 1), last[...]
-    dscores = attend_dscores(probs_ref[...], g, part(most, blocks + 1))
-    give(2, dv_in[...] + product(probs16_ref[...], g))
-    give(1, (dk_in[...] + product(dscores, q)) * SCALING)
-    give(0, (product(keys_t[...], dscores) * SCALING).T)
-    settle()
-
-
-def one_step(kernel, name, slot, inputs, held, shapes, cost):
+def one_step(kernel, name, slot, inputs, held, shapes, copies, cost):
     vmem = pl.BlockSpec(memory_space=pltpu.VMEM)
     anywhere = pl.BlockSpec(memory_space=pl.ANY)
     return pl.pallas_call(
@@ -288,8 +276,8 @@
         + [anywhere] * len(held),
         out_specs=(anywhere,) * len(held) + (vmem,) * len(shapes),
         scratch_shapes=[
-            pltpu.VMEM((3, SLOT, HEAD_DIM), jnp.bfloat16),
-            pltpu.SemaphoreType.DMA((3,)),
+            pltpu.VMEM((copies, SLOT, HEAD_DIM), jnp.bfloat16),
+            pltpu.SemaphoreType.DMA((copies,)),
         ],
         input_output_aliases={1 + len(inputs) + i: i for i in range(len(held))},
         compiler_params=pltpu.CompilerParams(vmem_limit_bytes=16 * 1024 * 1024),
@@ -301,7 +289,7 @@
 def body(query_rows, key_rows, value_rows, grad_rows, doc_ids, leaving_group):
     row_count, width = query_rows.shape
     heads = tuple(range(width // HEAD_DIM))
-    early, late = heads[:-2], heads[-2:]
+    early, late = heads[:-1], heads[-1:]
     group_count = row_count // SLOT
     far_bit = lax.axis_size("dp").bit_length() - 2
 
@@ -310,11 +298,8 @@
     )
     most, query_rows, grad_rows = lax.optimization_barrier((most, query_rows, grad_rows))
     most = swapped(most, "dp", far_bit)
-    mid = pack(leaving_group, late, late[:1], query_rows, grad_rows)
-    mid, query_rows, grad_rows = lax.optimization_barrier((mid, query_rows, grad_rows))
-    mid = swapped(mid, "dp", far_bit)
-    last = pack(leaving_group, (), late[1:], query_rows, grad_rows)
-    last = swapped(last, "dp", far_bit)
+    rest = pack(leaving_group, late, late, query_rows, grad_rows)
+    rest = swapped(rest, "dp", far_bit)
 
     ids = jnp.pad(doc_ids.reshape(group_count, RUNS, LANES), ((0, 0), (0, 8 - RUNS), (0, 0)))
     marks = jnp.concatenate([ids // 16, ids % 16], axis=1).astype(jnp.bfloat16)
@@ -339,47 +324,28 @@
     )
 
     pair_at = 2 * len(early)
-    marks_at = (pair_at + 2) * (SLOT // 16)
-
-    def marks_place(h, s):
-        return (marks_at, 0)
-
-    pair_places = (lambda h, s: (pair_at, 0), lambda h, s: (pair_at + 1, 0))
-    out, dq, dk_sum, dv_sum, keys_t, values_t = attend(
+    sum_shape = jax.ShapeDtypeStruct((SLOT, HEAD_DIM), jnp.float32)
+    flat_shape = jax.ShapeDtypeStruct((HEAD_DIM, SLOT), jnp.bfloat16)
+    out, dq, *sums = one_step(
+        functools.partial(early_kernel, early, pair_at),
+        "arrived_early",
         leaving_group,
-        early,
-        (most, most, most, most, most),
-        (
-            marks_place,
-            lambda h, s: (h, 0),
-            lambda h, s: (h + len(early), 0),
-            *pair_places,
-        ),
-        row_count,
-        width,
-        held=held[:2],
-    )
-    sum_shape = jax.ShapeDtypeStruct((SLOT, HEAD_DIM), jnp.float32)
-    square = [jax.ShapeDtypeStruct((SLOT, SLOT), t) for t in (jnp.float32, jnp.bfloat16)]
-    out, dq, *sums = one_step(
-        functools.partial(middle_kernel, late, pair_at),
-        "middle",
-        leaving_group,
-        (most, mid, dk_sum, dv_sum, keys_t, values_t),
-        (out, dq),
-        (sum_shape, sum_shape, *square),
-        2,
-    )
-    dq, dk, dv = one_step(
-        functools.partial(finish_kernel, late[1], pair_at),
+        (most,),
+        held[:2],
+        (sum_shape, sum_shape, flat_shape, flat_shape),
+        2 * len(early),
+        len(early),
+    )
+    return one_step(
+        functools.partial(finish_kernel, late[0], pair_at),
         "finish",
         leaving_group,
-        (most, mid, last, *sums, keys_t),
-        (dq, *held[2:]),
+        (most, rest, *sums),
+        (out, dq, *held[2:]),
         (),
+        4,
         1,
     )
-    return out, dq, dk, dv
 
 
 def solution(mesh):

time: 104 us -> 103 us (level)
  the two profiles are of different devices: /device:TPU:252 before, /device:TPU:254 now
where the time goes in v8:
time: 103 us
  waiting for transfers between devices  73.2 us (71%)
  starting transfers between devices  14.6 us (14%)
  Pallas kernels  14 us (14%)
  between operations  1.36 us (1%)
    ppermute x2, waiting for transfers between devices, swapped(): lax.ppermute(x, axis, [(i, i ^ 1 << bit) for i in range(lax.axis_size(axi...  73.2 us
    ppermute x2, starting transfers between devices, swapped(): lax.ppermute(x, axis, [(i, i ^ 1 << bit) for i in range(lax.axis_size(axi...  14.6 us
    pallas_call x1, Pallas kernels, attend(): pl.pallas_call(functools.partial(attend_kernel, len(heads)), out_shape=(w...  6.23 us
    pallas_call x2, Pallas kernels, one_step(): pl.pallas_call(kernel, out_shape=tuple((jax.ShapeDtypeStruct(x.shape, x.d...  4.6 us
    pallas_call x2, Pallas kernels, pack(): pl.pallas_call(functools.partial(pack_kernel, q_heads, g_heads, whole), o...  3.15 us
  transfers between devices with their start and end apart: 2, of which 2 were waited for; matrix products, arithmetic and copies ran while one was open for 0% of the time, Pallas kernels for 10%

profile of v8, /device:TPU:254, one launch (start us, length us, event | category | flops | bytes accessed | tf_op | source)
XLA Modules:
  0.0 103.2 jit_solution(13436654949171705056)
XLA Ops:
  1.3 2.2 %pack_8.1 = bf16[3088,128]{1,0:T(8,128)(2,1)S(1)} custom-call(s32[1]{0:T(128)S(6)} %copy.22.slot_ref, bf16[768,512]{1,0:T(8,128)(2,1)} %q_ref, bf16[768,512]{1,0:T(8,128)(2,1)} %g_ref, bf16[768,128]{1,0:T(8,128)(2,1)} %k_ref.1, bf16[768,128]{1,0:T(8,128)(2,1)} %v_ref.1, s32[768]{0:T(1024)} %refs_4_.1), custom_call_target="tpu_custom_call" | custom-call | tf_op jit(solution)/shard_map/pack_8/pallas_call | solution.py:96
  3.5 0.0 copy-start
  3.5 7.4 %collective-permute-start = (bf16[3088,128]{1,0:T(8,128)(2,1)S(1)}, bf16[3088,128]{1,0:T(8,128)(2,1)S(1)}, u32[]{:S(2)}, u32[]{:S(2)}) collective-permute-start(bf16[3088,128]{1,0:T(8,128)(2,1)S(1)} %pack_8.1), channel_id=1, source_target_pairs={{0,256},{8,264},{16,272},{24,280},{32,288},{40,296},{48,304},{56,3... | collective-permute-start | bytes 2371592 | tf_op jit(solution)/shard_map/ppermute | solution.py:24
  10.9 1.0 pack_2.1
  11.8 7.2 %collective-permute-start.1 = (bf16[768,128]{1,0:T(8,128)(2,1)S(1)}, bf16[768,128]{1,0:T(8,128)(2,1)S(1)}, u32[]{:S(2)}, u32[]{:S(2)}) collective-permute-start(bf16[768,128]{1,0:T(8,128)(2,1)S(1)} %pack_2.1), channel_id=1, source_target_pairs={{0,256},{8,264},{16,272},{24,280},{32,288},{40,296},{48,304},{56,3... | collective-permute-start | bytes 589832 | tf_op jit(solution)/shard_map/ppermute | solution.py:24
  19.0 0.0 copy-done
  19.1 6.2 %attend_staying.1 = (bf16[768,512]{1,0:T(8,128)(2,1)}, bf16[768,512]{1,0:T(8,128)(2,1)}, bf16[768,128]{1,0:T(8,128)(2,1)}, bf16[768,128]{1,0:T(8,128)(2,1)}) custom-call(s32[1]{0:T(128)S(6)} %sub.9.slot_ref, bf16[32,128]{1,0:T(8,128)(2,1)S(1)} %bitcast.1, bf16[768,512]{1,0:T(8,128)(2,1)} %q_ref, bf16[768,512]{1,0:T(8,128)(2,1)} %g_ref, ...), custom_call_target="tpu_custom_call" | custom-call | flops 905969664 | bytes 1966080 | tf_op jit(solution)/shard_map/attend_staying/pallas_call | solution.py:184
  25.3 66.7 %collective-permute-done.most = bf16[3088,128]{1,0:T(8,128)(2,1)S(1)} collective-permute-done((bf16[3088,128]{1,0:T(8,128)(2,1)S(1)}, bf16[3088,128]{1,0:T(8,128)(2,1)S(1)}, u32[]{:S(2)}, u32[]{:S(2)}) %collective-permute-start) | collective-permute-done | bytes 790560 | tf_op jit(solution)/shard_map/ppermute | solution.py:24
  92.0 2.9 %arrived_early.1 = (bf16[768,512]{1,0:T(8,128)(2,1)}, bf16[768,512]{1,0:T(8,128)(2,1)}, f32[384,128]{1,0:T(8,128)S(1)}, f32[384,128]{1,0:T(8,128)S(1)}, bf16[128...) custom-call(s32[1]{0:T(128)S(6)} %copy.22.slot_ref, ...), custom_call_target="tpu_custom_call", output_to_operand_aliasing={{0}: (2, {}), {1}: (3, {})} | custom-call | flops 679477248 | bytes 1572864 | tf_op jit(solution)/shard_map/arrived_early/pallas_call | solution.py:271
  94.9 6.5 %collective-permute-done.1.rest = bf16[768,128]{1,0:T(8,128)(2,1)S(1)} collective-permute-done((bf16[768,128]{1,0:T(8,128)(2,1)S(1)}, bf16[768,128]{1,0:T(8,128)(2,1)S(1)}, u32[]{:S(2)}, u32[]{:S(2)}) %collective-permute-start.1) | collective-permute-done | bytes 196640 | tf_op jit(solution)/shard_map/ppermute | solution.py:24
  101.5 1.7 %finish.1 = (bf16[768,512]{1,0:T(8,128)(2,1)}, bf16[768,512]{1,0:T(8,128)(2,1)}, bf16[768,128]{1,0:T(8,128)(2,1)}, bf16[768,128]{1,0:T(8,128)(2,1)}) custom-call(s32[1]{0:T(128)S(6)} %copy.22.slot_ref, bf16[3088,128]{1,0:T(8,128)(2,1)S(1)} %collective-permute-done.most, ...), custom_call_target="tpu_custom_call", output_to_operand_aliasing={{0}: (7, {}), {1}: (8, {}), {2}: (9, {}), {3}: (10, {})} | custom-call | flops 226492416 | bytes 786432 | tf_op jit(solution)/shard_map/finish/pallas_call | solution.py:271
  (3 shorter events, 0.0 us)
Async XLA Ops:
  3.5 15.6 %copy-start = (s32[768]{0:T(1024)S(1)}, s32[768]{0:T(1024)}, u32[]{:S(2)}) copy-start(s32[768]{0:T(1024)} %refs_4_.1) | copy-start | bytes 9220
  3.5 88.6 %collective-permute-start = (bf16[3088,128]{1,0:T(8,128)(2,1)S(1)}, bf16[3088,128]{1,0:T(8,128)(2,1)S(1)}, u32[]{:S(2)}, u32[]{:S(2)}) collective-permute-start(bf16[3088,128]{1,0:T(8,128)(2,1)S(1)} %pack_8.1), channel_id=1, source_target_pairs={{0,256},{8,264},{16,272},{24,280},{32,288},{40,296},{48,304},{56,3... | collective-permute-start | bytes 2371592 | tf_op jit(solution)/shard_map/ppermute | solution.py:24
  11.8 89.6 %collective-permute-start.1 = (bf16[768,128]{1,0:T(8,128)(2,1)S(1)}, bf16[768,128]{1,0:T(8,128)(2,1)S(1)}, u32[]{:S(2)}, u32[]{:S(2)}) collective-permute-start(bf16[768,128]{1,0:T(8,128)(2,1)S(1)} %pack_2.1), channel_id=1, source_target_pairs={{0,256},{8,264},{16,272},{24,280},{32,288},{40,296},{48,304},{56,3... | collective-permute-start | bytes 589832 | tf_op jit(solution)/shard_map/ppermute | solution.py:24

commit v9 on v8

--- a/solution.py
+++ b/solution.py
@@ -104,14 +104,17 @@
     )(slot, *inputs)
 
 
-def attend_probs(ids, q, keys):
-    scores = lax.dot_general(keys, q, OVER_LANES, preferred_element_type=jnp.float32)
+def allowed_of(ids):
     ids_t = ids.T
     key_ids = jnp.concatenate([ids_t[:, j : j + 1] for j in range(RUNS)], axis=0)
     row_ids = jnp.concatenate([ids[j : j + 1, :] for j in range(RUNS)], axis=1)
     key_places = lax.broadcasted_iota(jnp.int32, (SLOT, SLOT), 0)
     row_places = lax.broadcasted_iota(jnp.int32, (SLOT, SLOT), 1)
-    allowed = (key_ids == row_ids) & (key_places <= row_places)
+    return (key_ids == row_ids) & (key_places <= row_places)
+
+
+def attend_probs(allowed, q, keys):
+    scores = lax.dot_general(keys, q, OVER_LANES, preferred_element_type=jnp.float32)
     scores = jnp.where(allowed, scores * (SCALING * LOG2E), MASKED)
     weights = jnp.exp2(scores - jnp.max(scores, axis=0, keepdims=True))
     return weights * (1.0 / jnp.sum(weights, axis=0, keepdims=True))
@@ -124,7 +127,7 @@
 
 
 def attend_head(ids, q, g, keys, values, keys_t, values_t):
-    probs = attend_probs(ids, q, keys)
+    probs = attend_probs(allowed_of(ids), q, keys)
     probs16 = probs.astype(jnp.bfloat16)
     dscores = attend_dscores(probs, g, values)
     dv = jnp.dot(probs16, g, preferred_element_type=jnp.float32)
@@ -227,17 +230,17 @@
 
 
 def early_kernel(heads, blocks, slot_ref, most, *refs):
-    o_ref, dq_ref, dk_ref, dv_ref, keys_t, values_t, made, sems = refs[2:]
+    o_ref, dq_ref, dk_ref, dv_ref, keys_t, values_t, mask, made, sems = refs[2:]
     rows = pl.ds(pl.multiple_of(slot_ref[0] * SLOT, SLOT), SLOT)
     places = [ref.at[rows, lanes(h)] for h in heads for ref in (o_ref, dq_ref)]
     give, settle = giver(made, places, sems)
     keys, values = part(most, blocks), part(most, blocks + 1)
-    ids = numbers(most[(blocks + 2) * SLOT :, :])
+    mask[...] = allowed_of(numbers(most[(blocks + 2) * SLOT :, :])).astype(jnp.float32)
     keys_t[...] = keys.T
     values_t[...] = values.T
     for i in range(len(heads)):
         q, g = part(most, i), part(most, len(heads) + i)
-        probs = attend_probs(ids, q, keys)
+        probs = attend_probs(mask[...] > 0.5, q, keys)
         probs16 = probs.astype(jnp.bfloat16)
         dscores = attend_dscores(probs, g, values)
         give(2 * i, product(values_t[...], probs16).T)
@@ -248,14 +251,15 @@
     settle()
 
 
-def finish_kernel(head, blocks, slot_ref, most, rest, dk_in, dv_in, keys_t, values_t, *refs):
+def finish_kernel(
+    head, blocks, slot_ref, most, rest, dk_in, dv_in, keys_t, values_t, mask, *refs
+):
     o_ref, dq_ref, dk_ref, dv_ref, made, sems = refs[4:]
     rows = pl.ds(pl.multiple_of(slot_ref[0] * SLOT, SLOT), SLOT)
     places = (o_ref.at[rows, lanes(head)], dq_ref.at[rows, lanes(head)])
     give, settle = giver(made, places + (dk_ref.at[rows], dv_ref.at[rows]), sems)
-    ids = numbers(most[(blocks + 2) * SLOT :, :])
     q, g = part(rest, 0), part(rest, 1)
-    probs = attend_probs(ids, q, part(most, blocks))
+    probs = attend_probs(mask[...] > 0.5, q, part(most, blocks))
     probs16 = probs.astype(jnp.bfloat16)
     dscores = attend_dscores(probs, g, part(most, blocks + 1))
     give(3, dv_in[...] + product(probs16, g))
@@ -326,13 +330,14 @@
     pair_at = 2 * len(early)
     sum_shape = jax.ShapeDtypeStruct((SLOT, HEAD_DIM), jnp.float32)
     flat_shape = jax.ShapeDtypeStruct((HEAD_DIM, SLOT), jnp.bfloat16)
+    square = jax.ShapeDtypeStruct((SLOT, SLOT), jnp.float32)
     out, dq, *sums = one_step(
         functools.partial(early_kernel, early, pair_at),
         "arrived_early",
         leaving_group,
         (most,),
         held[:2],
-        (sum_shape, sum_shape, flat_shape, flat_shape),
+        (sum_shape, sum_shape, flat_shape, flat_shape, square),
         2 * len(early),
         len(early),
     )

time: 103 us -> 103 us (level)
  the two profiles are of different devices: /device:TPU:254 before, /device:TPU:238 now
where the time goes in v9:
time: 103 us
  waiting for transfers between devices  73 us (71%)
  starting transfers between devices  14.6 us (14%)
  Pallas kernels  14.1 us (14%)
  between operations  1.36 us (1%)
    ppermute x2, waiting for transfers between devices, swapped(): lax.ppermute(x, axis, [(i, i ^ 1 << bit) for i in range(lax.axis_size(axi...  73 us
    ppermute x2, starting transfers between devices, swapped(): lax.ppermute(x, axis, [(i, i ^ 1 << bit) for i in range(lax.axis_size(axi...  14.6 us
    pallas_call x1, Pallas kernels, attend(): pl.pallas_call(functools.partial(attend_kernel, len(heads)), out_shape=(w...  6.22 us
    pallas_call x2, Pallas kernels, one_step(): pl.pallas_call(kernel, out_shape=tuple((jax.ShapeDtypeStruct(x.shape, x.d...  4.75 us
    pallas_call x2, Pallas kernels, pack(): pl.pallas_call(functools.partial(pack_kernel, q_heads, g_heads, whole), o...  3.15 us
  transfers between devices with their start and end apart: 2, of which 2 were waited for; matrix products, arithmetic and copies ran while one was open for 0% of the time, Pallas kernels for 10%

profile of v9, /device:TPU:238, one launch (start us, length us, event | category | flops | bytes accessed | tf_op | source)
XLA Modules:
  0.0 103.1 jit_solution(17786772566580916655)
XLA Ops:
  1.3 2.2 %pack_8.1 = bf16[3088,128]{1,0:T(8,128)(2,1)S(1)} custom-call(s32[1]{0:T(128)S(6)} %copy.22.slot_ref, bf16[768,512]{1,0:T(8,128)(2,1)} %q_ref, bf16[768,512]{1,0:T(8,128)(2,1)} %g_ref, bf16[768,128]{1,0:T(8,128)(2,1)} %k_ref.1, bf16[768,128]{1,0:T(8,128)(2,1)} %v_ref.1, s32[768]{0:T(1024)} %refs_4_.1), custom_call_target="tpu_custom_call" | custom-call | tf_op jit(solution)/shard_map/pack_8/pallas_call | solution.py:96
  3.5 0.0 copy-start
  3.5 7.4 %collective-permute-start = (bf16[3088,128]{1,0:T(8,128)(2,1)S(1)}, bf16[3088,128]{1,0:T(8,128)(2,1)S(1)}, u32[]{:S(2)}, u32[]{:S(2)}) collective-permute-start(bf16[3088,128]{1,0:T(8,128)(2,1)S(1)} %pack_8.1), channel_id=1, source_target_pairs={{0,256},{8,264},{16,272},{24,280},{32,288},{40,296},{48,304},{56,3... | collective-permute-start | bytes 2371592 | tf_op jit(solution)/shard_map/ppermute | solution.py:24
  10.9 1.0 pack_2.1
  11.8 7.2 %collective-permute-start.1 = (bf16[768,128]{1,0:T(8,128)(2,1)S(1)}, bf16[768,128]{1,0:T(8,128)(2,1)S(1)}, u32[]{:S(2)}, u32[]{:S(2)}) collective-permute-start(bf16[768,128]{1,0:T(8,128)(2,1)S(1)} %pack_2.1), channel_id=1, source_target_pairs={{0,256},{8,264},{16,272},{24,280},{32,288},{40,296},{48,304},{56,3... | collective-permute-start | bytes 589832 | tf_op jit(solution)/shard_map/ppermute | solution.py:24
  19.0 0.0 copy-done
  19.1 6.2 %attend_staying.1 = (bf16[768,512]{1,0:T(8,128)(2,1)}, bf16[768,512]{1,0:T(8,128)(2,1)}, bf16[768,128]{1,0:T(8,128)(2,1)}, bf16[768,128]{1,0:T(8,128)(2,1)}) custom-call(s32[1]{0:T(128)S(6)} %sub.9.slot_ref, bf16[32,128]{1,0:T(8,128)(2,1)S(1)} %bitcast.1, bf16[768,512]{1,0:T(8,128)(2,1)} %q_ref, bf16[768,512]{1,0:T(8,128)(2,1)} %g_ref, ...), custom_call_target="tpu_custom_call" | custom-call | flops 905969664 | bytes 1966080 | tf_op jit(solution)/shard_map/attend_staying/pallas_call | solution.py:187
  25.3 66.7 %collective-permute-done.most = bf16[3088,128]{1,0:T(8,128)(2,1)S(1)} collective-permute-done((bf16[3088,128]{1,0:T(8,128)(2,1)S(1)}, bf16[3088,128]{1,0:T(8,128)(2,1)S(1)}, u32[]{:S(2)}, u32[]{:S(2)}) %collective-permute-start) | collective-permute-done | bytes 790560 | tf_op jit(solution)/shard_map/ppermute | solution.py:24
  92.0 3.1 %arrived_early.1 = (bf16[768,512]{1,0:T(8,128)(2,1)}, bf16[768,512]{1,0:T(8,128)(2,1)}, f32[384,128]{1,0:T(8,128)S(1)}, f32[384,128]{1,0:T(8,128)S(1)}, bf16[128...) custom-call(s32[1]{0:T(128)S(6)} %copy.22.slot_ref, ...), custom_call_target="tpu_custom_call", output_to_operand_aliasing={{0}: (2, {}), {1}: (3, {})} | custom-call | flops 679477248 | bytes 1572864 | tf_op jit(solution)/shard_map/arrived_early/pallas_call | solution.py:275
  95.2 6.3 %collective-permute-done.1.rest = bf16[768,128]{1,0:T(8,128)(2,1)S(1)} collective-permute-done((bf16[768,128]{1,0:T(8,128)(2,1)S(1)}, bf16[768,128]{1,0:T(8,128)(2,1)S(1)}, u32[]{:S(2)}, u32[]{:S(2)}) %collective-permute-start.1) | collective-permute-done | bytes 196640 | tf_op jit(solution)/shard_map/ppermute | solution.py:24
  101.5 1.6 %finish.1 = (bf16[768,512]{1,0:T(8,128)(2,1)}, bf16[768,512]{1,0:T(8,128)(2,1)}, bf16[768,128]{1,0:T(8,128)(2,1)}, bf16[768,128]{1,0:T(8,128)(2,1)}) custom-call(s32[1]{0:T(128)S(6)} %copy.22.slot_ref, bf16[3088,128]{1,0:T(8,128)(2,1)S(1)} %collective-permute-done.most, ...), custom_call_target="tpu_custom_call", output_to_operand_aliasing={{0}: (8, {}), {1}: (9, {}), {2}: (10, {}), {3}: (11, {})} | custom-call | flops 226492416 | bytes 786432 | tf_op jit(solution)/shard_map/finish/pallas_call | solution.py:275
  (3 shorter events, 0.0 us)
Async XLA Ops:
  3.5 15.6 %copy-start = (s32[768]{0:T(1024)S(1)}, s32[768]{0:T(1024)}, u32[]{:S(2)}) copy-start(s32[768]{0:T(1024)} %refs_4_.1) | copy-start | bytes 9220
  3.5 88.6 %collective-permute-start = (bf16[3088,128]{1,0:T(8,128)(2,1)S(1)}, bf16[3088,128]{1,0:T(8,128)(2,1)S(1)}, u32[]{:S(2)}, u32[]{:S(2)}) collective-permute-start(bf16[3088,128]{1,0:T(8,128)(2,1)S(1)} %pack_8.1), channel_id=1, source_target_pairs={{0,256},{8,264},{16,272},{24,280},{32,288},{40,296},{48,304},{56,3... | collective-permute-start | bytes 2371592 | tf_op jit(solution)/shard_map/ppermute | solution.py:24
  11.8 89.6 %collective-permute-start.1 = (bf16[768,128]{1,0:T(8,128)(2,1)S(1)}, bf16[768,128]{1,0:T(8,128)(2,1)S(1)}, u32[]{:S(2)}, u32[]{:S(2)}) collective-permute-start(bf16[768,128]{1,0:T(8,128)(2,1)S(1)} %pack_2.1), channel_id=1, source_target_pairs={{0,256},{8,264},{16,272},{24,280},{32,288},{40,296},{48,304},{56,3... | collective-permute-start | bytes 589832 | tf_op jit(solution)/shard_map/ppermute | solution.py:24

commit v10 on v9

--- a/solution.py
+++ b/solution.py
@@ -264,8 +264,8 @@
     dscores = attend_dscores(probs, g, part(most, blocks + 1))
     give(3, dv_in[...] + product(probs16, g))
     give(0, product(values_t[...], probs16).T)
+    give(1, (product(keys_t[...], dscores) * SCALING).T)
     give(2, (dk_in[...] + product(dscores, q)) * SCALING)
-    give(1, (product(keys_t[...], dscores) * SCALING).T)
     settle()
 
 

time: 103 us -> 103 us (level)
  the two profiles are of different devices: /device:TPU:238 before, /device:TPU:246 now
where the time goes in v10:
time: 103 us
  waiting for transfers between devices  73 us (71%)
  starting transfers between devices  14.6 us (14%)
  Pallas kernels  14.1 us (14%)
  between operations  1.36 us (1%)
    ppermute x2, waiting for transfers between devices, swapped(): lax.ppermute(x, axis, [(i, i ^ 1 << bit) for i in range(lax.axis_size(axi...  73 us
    ppermute x2, starting transfers between devices, swapped(): lax.ppermute(x, axis, [(i, i ^ 1 << bit) for i in range(lax.axis_size(axi...  14.6 us
    pallas_call x1, Pallas kernels, attend(): pl.pallas_call(functools.partial(attend_kernel, len(heads)), out_shape=(w...  6.21 us
    pallas_call x2, Pallas kernels, one_step(): pl.pallas_call(kernel, out_shape=tuple((jax.ShapeDtypeStruct(x.shape, x.d...  4.73 us
    pallas_call x2, Pallas kernels, pack(): pl.pallas_call(functools.partial(pack_kernel, q_heads, g_heads, whole), o...  3.15 us
  transfers between devices with their start and end apart: 2, of which 2 were waited for; matrix products, arithmetic and copies ran while one was open for 0% of the time, Pallas kernels for 10%

profile of v10, /device:TPU:246, one launch (start us, length us, event | category | flops | bytes accessed | tf_op | source)
XLA Modules:
  0.0 103.1 jit_solution(9793266763090523959)
XLA Ops:
  1.3 2.2 %pack_8.1 = bf16[3088,128]{1,0:T(8,128)(2,1)S(1)} custom-call(s32[1]{0:T(128)S(6)} %copy.22.slot_ref, bf16[768,512]{1,0:T(8,128)(2,1)} %q_ref, bf16[768,512]{1,0:T(8,128)(2,1)} %g_ref, bf16[768,128]{1,0:T(8,128)(2,1)} %k_ref.1, bf16[768,128]{1,0:T(8,128)(2,1)} %v_ref.1, s32[768]{0:T(1024)} %refs_4_.1), custom_call_target="tpu_custom_call" | custom-call | tf_op jit(solution)/shard_map/pack_8/pallas_call | solution.py:96
  3.5 0.0 copy-start
  3.5 7.4 %collective-permute-start = (bf16[3088,128]{1,0:T(8,128)(2,1)S(1)}, bf16[3088,128]{1,0:T(8,128)(2,1)S(1)}, u32[]{:S(2)}, u32[]{:S(2)}) collective-permute-start(bf16[3088,128]{1,0:T(8,128)(2,1)S(1)} %pack_8.1), channel_id=1, source_target_pairs={{0,256},{8,264},{16,272},{24,280},{32,288},{40,296},{48,304},{56,3... | collective-permute-start | bytes 2371592 | tf_op jit(solution)/shard_map/ppermute | solution.py:24
  10.9 1.0 pack_2.1
  11.8 7.2 %collective-permute-start.1 = (bf16[768,128]{1,0:T(8,128)(2,1)S(1)}, bf16[768,128]{1,0:T(8,128)(2,1)S(1)}, u32[]{:S(2)}, u32[]{:S(2)}) collective-permute-start(bf16[768,128]{1,0:T(8,128)(2,1)S(1)} %pack_2.1), channel_id=1, source_target_pairs={{0,256},{8,264},{16,272},{24,280},{32,288},{40,296},{48,304},{56,3... | collective-permute-start | bytes 589832 | tf_op jit(solution)/shard_map/ppermute | solution.py:24
  19.0 0.0 copy-done
  19.1 6.2 %attend_staying.1 = (bf16[768,512]{1,0:T(8,128)(2,1)}, bf16[768,512]{1,0:T(8,128)(2,1)}, bf16[768,128]{1,0:T(8,128)(2,1)}, bf16[768,128]{1,0:T(8,128)(2,1)}) custom-call(s32[1]{0:T(128)S(6)} %sub.9.slot_ref, bf16[32,128]{1,0:T(8,128)(2,1)S(1)} %bitcast.1, bf16[768,512]{1,0:T(8,128)(2,1)} %q_ref, bf16[768,512]{1,0:T(8,128)(2,1)} %g_ref, ...), custom_call_target="tpu_custom_call" | custom-call | flops 905969664 | bytes 1966080 | tf_op jit(solution)/shard_map/attend_staying/pallas_call | solution.py:187
  25.3 66.7 %collective-permute-done.most = bf16[3088,128]{1,0:T(8,128)(2,1)S(1)} collective-permute-done((bf16[3088,128]{1,0:T(8,128)(2,1)S(1)}, bf16[3088,128]{1,0:T(8,128)(2,1)S(1)}, u32[]{:S(2)}, u32[]{:S(2)}) %collective-permute-start) | collective-permute-done | bytes 790560 | tf_op jit(solution)/shard_map/ppermute | solution.py:24
  92.0 3.1 %arrived_early.1 = (bf16[768,512]{1,0:T(8,128)(2,1)}, bf16[768,512]{1,0:T(8,128)(2,1)}, f32[384,128]{1,0:T(8,128)S(1)}, f32[384,128]{1,0:T(8,128)S(1)}, bf16[128...) custom-call(s32[1]{0:T(128)S(6)} %copy.22.slot_ref, ...), custom_call_target="tpu_custom_call", output_to_operand_aliasing={{0}: (2, {}), {1}: (3, {})} | custom-call | flops 679477248 | bytes 1572864 | tf_op jit(solution)/shard_map/arrived_early/pallas_call | solution.py:275
  95.2 6.3 %collective-permute-done.1.rest = bf16[768,128]{1,0:T(8,128)(2,1)S(1)} collective-permute-done((bf16[768,128]{1,0:T(8,128)(2,1)S(1)}, bf16[768,128]{1,0:T(8,128)(2,1)S(1)}, u32[]{:S(2)}, u32[]{:S(2)}) %collective-permute-start.1) | collective-permute-done | bytes 196640 | tf_op jit(solution)/shard_map/ppermute | solution.py:24
  101.5 1.6 %finish.1 = (bf16[768,512]{1,0:T(8,128)(2,1)}, bf16[768,512]{1,0:T(8,128)(2,1)}, bf16[768,128]{1,0:T(8,128)(2,1)}, bf16[768,128]{1,0:T(8,128)(2,1)}) custom-call(s32[1]{0:T(128)S(6)} %copy.22.slot_ref, bf16[3088,128]{1,0:T(8,128)(2,1)S(1)} %collective-permute-done.most, ...), custom_call_target="tpu_custom_call", output_to_operand_aliasing={{0}: (8, {}), {1}: (9, {}), {2}: (10, {}), {3}: (11, {})} | custom-call | flops 226492416 | bytes 786432 | tf_op jit(solution)/shard_map/finish/pallas_call | solution.py:275
  (3 shorter events, 0.0 us)
Async XLA Ops:
  3.5 15.6 %copy-start = (s32[768]{0:T(1024)S(1)}, s32[768]{0:T(1024)}, u32[]{:S(2)}) copy-start(s32[768]{0:T(1024)} %refs_4_.1) | copy-start | bytes 9220
  3.5 88.6 %collective-permute-start = (bf16[3088,128]{1,0:T(8,128)(2,1)S(1)}, bf16[3088,128]{1,0:T(8,128)(2,1)S(1)}, u32[]{:S(2)}, u32[]{:S(2)}) collective-permute-start(bf16[3088,128]{1,0:T(8,128)(2,1)S(1)} %pack_8.1), channel_id=1, source_target_pairs={{0,256},{8,264},{16,272},{24,280},{32,288},{40,296},{48,304},{56,3... | collective-permute-start | bytes 2371592 | tf_op jit(solution)/shard_map/ppermute | solution.py:24
  11.8 89.6 %collective-permute-start.1 = (bf16[768,128]{1,0:T(8,128)(2,1)S(1)}, bf16[768,128]{1,0:T(8,128)(2,1)S(1)}, u32[]{:S(2)}, u32[]{:S(2)}) collective-permute-start(bf16[768,128]{1,0:T(8,128)(2,1)S(1)} %pack_2.1), channel_id=1, source_target_pairs={{0,256},{8,264},{16,272},{24,280},{32,288},{40,296},{48,304},{56,3... | collective-permute-start | bytes 589832 | tf_op jit(solution)/shard_map/ppermute | solution.py:24
